TPU v7x, 256 devices: a whole 4x4x8 slice. The times are simulated.
256 devices in a mesh: dom: 32 (over y, z), feat: 8 (over x, core).
Axes of the slice: x: 4, y: 4, z: 8, core: 2. Of those that a mesh axis runs over, the one named last changes fastest.
Arguments:
- node_feats: bfloat16 [262144, 128], P(('dom', 'feat')), may hold values from -6 to 6
- cached_feats: bfloat16 [131072, 128], P(('dom', 'feat')), may hold values from -6 to 6
- tile_values: bfloat16 [65536, 128, 128], P(('dom', 'feat')), may hold values from -0.125 to 0.125
- tile_row: int32 [256, 256], P(('dom', 'feat')), may hold values from 0 to 7
- tile_col: int32 [256, 256], P(('dom', 'feat')), may hold values from 0 to 75
- tile_count: int32 [256], P(('dom', 'feat')), may hold values from 1 to 256, as said below
- need_blocks: int32 [256, 32, 2], P(('dom', 'feat')), may hold values from 0 to 11
- weights: bfloat16 [128, 128], replicated, may hold values from -0.5 to 0.5
- grad_out: bfloat16 [262144, 128], P(('dom', 'feat')), may hold values from -6 to 6
Outputs:
- output: bfloat16 [262144, 128], P(('dom', 'feat'))
- h_grad: bfloat16 [262144, 128], P(('dom', 'feat'))
- w_grad: float32 [128, 128], replicated
Inputs may be any that keep to these rules, and one draw needn't show every extreme that they name: `tile_count`: slots at or beyond a device's count are unused; some device uses all 256 slots. `tile_row`: local row block of each slot. `tile_col`: below 12: one of the device's own source blocks; else 12 + p * 2 + s names slot s of the blocks taken from partition p of the same batch. need_blocks[g, p, s] is a source block of partition p of device g's batch.
All inputs are finite; a program needn't handle non-finite values.
Results may differ from a plain program's by a relative error of at most 0.0061.
Values may be sent and summed in bfloat16 or wider, within the bound.
A program may use at most 128 MiB of HBM per device.

v0:
```python
import math

import jax
import jax.numpy as jnp
from jax import lax
from jax.sharding import PartitionSpec as P


def body(
    node_feats,
    cached_feats,
    tile_values,
    tile_row,
    tile_col,
    tile_count,
    need_blocks,
    weights,
    grad_out,
):
    tile_size = tile_values.shape[1]
    feat_width = node_feats.shape[1]
    blocks = node_feats.shape[0] // tile_size
    sources = jnp.concatenate(
        [
            node_feats.reshape(blocks, tile_size, feat_width),
            cached_feats.reshape(-1, tile_size, feat_width),
        ],
        axis=0,
    )
    src_count = sources.shape[0]
    peer_count = lax.axis_size("dom")
    slot_count = need_blocks.shape[2]
    wanted = need_blocks[0]
    capacity = tile_values.shape[0]
    row_ids = tile_row[0]
    col_ids = tile_col[0]
    active = (jnp.arange(capacity, dtype=jnp.int32) < tile_count[0]).astype(jnp.float32)
    source_table = lax.all_gather(sources, "dom", axis=0, tiled=True)
    my_index = lax.axis_index("dom")
    local_ids = my_index * src_count + jnp.arange(src_count, dtype=jnp.int32)
    remote_ids = (jnp.arange(peer_count, dtype=jnp.int32)[:, None] * src_count + wanted).reshape(-1)
    column_ref = jnp.concatenate([local_ids, remote_ids])[col_ids]
    group_size = math.gcd(capacity, 32)
    group_count = capacity // group_size
    tile_groups = tile_values.reshape(group_count, group_size, tile_size, tile_size)
    row_groups = row_ids.reshape(group_count, group_size)
    mask_groups = active.reshape(group_count, group_size)

    def forward_step(total, packed):
        tile_group, refs, targets, mask = packed
        picked = source_table[refs]
        product = jnp.einsum("tij,tjf->tif", tile_group, picked, preferred_element_type=jnp.float32)
        return (total.at[targets].add(product * mask[:, None, None]), None)

    start = jnp.zeros((blocks, tile_size, feat_width), jnp.float32)
    summed, unused = lax.scan(
        forward_step,
        start,
        (tile_groups, column_ref.reshape(group_count, group_size), row_groups, mask_groups),
    )
    mixed = summed.astype(jnp.bfloat16).reshape(blocks * tile_size, feat_width)
    pre_act = jnp.dot(mixed, weights, preferred_element_type=jnp.float32)
    sigmoid_vals = jax.nn.sigmoid(pre_act)
    output = (pre_act * sigmoid_vals).astype(jnp.bfloat16)
    act_grad = (
        grad_out.astype(jnp.float32) * sigmoid_vals * (1.0 + pre_act * (1.0 - sigmoid_vals))
    ).astype(jnp.bfloat16)
    mixed_grad = jnp.dot(act_grad, weights.T, preferred_element_type=jnp.float32).astype(
        jnp.bfloat16
    )
    grad_blocks = mixed_grad.reshape(blocks, tile_size, feat_width)

    def backward_step(total, packed):
        tile_group, refs, targets, mask = packed
        picked = grad_blocks[targets]
        product = jnp.einsum("tij,tif->tjf", tile_group, picked, preferred_element_type=jnp.float32)
        return (total.at[refs].add(product * mask[:, None, None]), None)

    column_total = src_count + peer_count * slot_count
    start_back = jnp.zeros((column_total, tile_size, feat_width), jnp.float32)
    spread_total, unused_back = lax.scan(
        backward_step,
        start_back,
        (tile_groups, col_ids.reshape(group_count, group_size), row_groups, mask_groups),
    )
    local_part = spread_total[:blocks]
    slot_part = spread_total[src_count:].reshape(peer_count, slot_count, tile_size, feat_width)
    targets_all = jnp.arange(peer_count, dtype=jnp.int32)[:, None] * blocks + wanted
    targets_all = jnp.where(wanted < blocks, targets_all, peer_count * blocks).reshape(-1)
    spread = (
        jnp.zeros((peer_count * blocks, tile_size, feat_width), jnp.float32)
        .at[targets_all]
        .add(slot_part.reshape(-1, tile_size, feat_width), mode="drop")
    )
    remote = lax.psum_scatter(spread, "dom", scatter_dimension=0, tiled=True)
    h_grad = (local_part + remote).astype(jnp.bfloat16).reshape(blocks * tile_size, feat_width)
    local_weight = lax.dot_general(
        mixed, act_grad, (((0,), (0,)), ((), ())), preferred_element_type=jnp.float32
    )
    total_nodes = blocks * tile_size * peer_count * lax.axis_size("feat")
    w_grad = lax.psum(local_weight, ("dom", "feat")) * (1.0 / math.sqrt(total_nodes))
    return (output, h_grad, w_grad)


def solution(mesh):
    in_specs = (
        P(("dom", "feat"), None),
        P(("dom", "feat"), None),
        P(("dom", "feat"), None, None),
        P(("dom", "feat"), None),
        P(("dom", "feat"), None),
        P(("dom", "feat")),
        P(("dom", "feat"), None, None),
        P(),
        P(("dom", "feat"), None),
    )
    out_specs = (P(("dom", "feat"), None), P(("dom", "feat"), None), P())
    return jax.shard_map(body, mesh=mesh, in_specs=in_specs, out_specs=out_specs, check_vma=False)
```

profile of v0, /device:TPU:2, one launch (start us, length us, event | category | flops | bytes accessed | tf_op | source)
XLA Modules:
  0.0 711.9 jit_solution(16314038345252234004)
XLA Ops:
  7.2 1.8 pad_maximum_fusion
  15.3 1.9 gather_fusion.2
  17.2 12.0 %copy.20 = bf16[256,128,128]{1,2,0:T(8,128)(2,1)} copy(bf16[256,128,128]{2,1,0:T(8,128)(2,1)} %param.15) | data formatting | bytes 16777216 | tf_op args[2]
  29.2 104.1 %all-gather.2.cloned.1.call-done = bf16[384,128,128]{2,1,0:T(8,128)(2,1)} async-done(((bf16[12,128,128]{2,1,0:T(8,128)(2,1)}), bf16[384,128,128]{2,1,0:T(8,128)(2,1)}) %all-gather.2.cloned.1.call-update) | async-done | bytes 12582928 | tf_op jit(solution)/shard_map/all_gather | solution.py:38
  133.3 87.6 %while.20 = (s32[]{:T(128)}, f32[8,128,128]{2,1,0:T(8,128)S(1)}, s32[8,32]{1,0:T(8,128)S(1)}, bf16[8,32,128,128]{3,2,1,0:T(8,128)(2,1)}, s32[8,32]{1,0:T(8,128)S...) while((s32[]{:T(128)}, f32[8,128,128]{2,1,0:T(8,128)S(1)}, ...), condition=%wide.region_2.3_spmd, body=%wide.region_0.2_spmd.sunk | while | flops 135267520 | bytes 12588393 | solution.py:56
  133.4 6.3 gather_fusion
  139.7 2.0 convolution_multiply_fusion.4
  141.6 2.7 scatter_fusion
  144.4 6.2 gather_fusion
  150.6 2.0 convolution_multiply_fusion.4
  152.6 2.7 scatter_fusion
  155.3 6.2 gather_fusion
  161.5 2.0 convolution_multiply_fusion.4
  163.5 2.7 scatter_fusion
  166.2 6.2 gather_fusion
  172.5 2.0 convolution_multiply_fusion.4
  174.5 2.7 scatter_fusion
  177.2 6.2 gather_fusion
  183.4 2.0 convolution_multiply_fusion.4
  185.4 2.7 scatter_fusion
  188.1 6.2 gather_fusion
  194.4 2.0 convolution_multiply_fusion.4
  196.3 2.7 scatter_fusion
  199.1 6.2 gather_fusion
  205.3 2.0 convolution_multiply_fusion.4
  207.3 2.7 scatter_fusion
  210.0 6.2 gather_fusion
  216.2 2.0 convolution_multiply_fusion.4
  218.2 2.7 scatter_fusion
  223.3 2.9 broadcast_in_dim.13
  226.2 69.2 %while.21 = (s32[]{:T(128)}, f32[76,128,128]{2,1,0:T(8,128)}, s32[8,32]{1,0:T(8,128)S(1)}, bf16[8,32,128,128]{2,3,1,0:T(8,128)(2,1)}, s32[8,32]{1,0:T(8,128)S(1)...) while((s32[]{:T(128)}, f32[76,128,128]{2,1,0:T(8,128)}, s32[8,32]{1,0:T(8,128)S(1)}, ...), condition=%wide.region_5.6_spmd, body=%wide.region_3.5_spmd.sunk | while | flops 135267520 | bytes 12588393 | solution.py:81
  228.6 6.2 scatter_fusion.1
  235.6 1.7 convolution_multiply_fusion.5
  237.3 6.2 scatter_fusion.1
  245.9 6.2 scatter_fusion.1
  252.9 1.7 convolution_multiply_fusion.5
  254.6 6.2 scatter_fusion.1
  263.2 6.2 scatter_fusion.1
  270.2 1.7 convolution_multiply_fusion.5
  271.8 6.2 scatter_fusion.1
  280.5 6.2 scatter_fusion.1
  289.1 6.2 scatter_fusion.1
  295.4 4.6 slice.7
  300.0 7.8 %broadcast_in_dim.17 = f32[256,128,128]{2,1,0:T(8,128)} broadcast(f32[]{:T(128)} %constant.19.clone.1), dimensions={} | broadcast | bytes 16777220 | tf_op jit(solution)/shard_map/broadcast_in_dim | solution.py:91
  307.8 13.3 %scatter_fusion.2 = f32[256,128,128]{2,1,0:T(8,128)} fusion(f32[256,128,128]{2,1,0:T(8,128)} %broadcast_in_dim.17, s32[64]{0:T(128)S(1)} %fusion.17, f32[64,128,128]{2,1,0:T(8,128)} %slice.7), kind=kCustom, calls=%fused_computation.5 | custom fusion | flops 1048576 | bytes 12583168 | tf_op jit(solution)/shard_map/scatter-add | solution.py:93
  321.1 136.1 %all-reduce.2.cloned.1.call-done = f32[128,128]{1,0:T(8,128)} async-done(((f32[128,128]{1,0:T(8,128)}), f32[128,128]{1,0:T(8,128)}) %all-reduce.2.cloned.1.call-update) | async-done | bytes 65552 | tf_op jit(solution)/shard_map/psum | solution.py:101
  458.7 244.8 %reduce-scatter.2.cloned.1.call-done = f32[8,128,128]{2,1,0:T(8,128)} async-done(((f32[256,128,128]{2,1,0:T(8,128)}), f32[8,128,128]{2,1,0:T(8,128)}) %reduce-scatter.2.cloned.1.call-update) | async-done | bytes 524304 | tf_op jit(solution)/shard_map/reduce_scatter | solution.py:95
  703.5 2.0 add_convert_fusion
  (99 shorter events, 24.2 us)
Async XLA Ops:
  7.2 213.8 %copy-start = (bf16[128,128]{1,0:T(8,128)(2,1)S(1)}, bf16[128,128]{1,0:T(8,128)(2,1)}, u32[]{:S(2)}) copy-start(bf16[128,128]{1,0:T(8,128)(2,1)} %param.20) | copy-start | bytes 98308
  7.2 126.1 %all-gather.2.cloned.1.call-start = ((), (), s32[]{:S(2)}) async-start(), calls=%async_computation.1 | async-start | bytes 12976128 | tf_op jit(solution)/shard_map/all_gather | solution.py:38
  9.1 448.1 %all-reduce.2.cloned.1.call-start = ((), (), s32[]{:S(2)}) async-start(), calls=%async_computation.3 | async-start | bytes 131072 | tf_op jit(solution)/shard_map/psum | solution.py:101
  133.3 87.6 %copy-start.1 = (bf16[1024,128]{1,0:T(8,128)(2,1)S(1)}, bf16[1024,128]{1,0:T(8,128)(2,1)}, u32[]{:S(2)}) copy-start(bf16[1024,128]{1,0:T(8,128)(2,1)} %param.21) | copy-start | bytes 786436
  223.2 480.2 %reduce-scatter.2.cloned.1.call-start = ((), (), s32[]{:S(2)}) async-start(), calls=%async_computation.2 | async-start | bytes 17301504 | tf_op jit(solution)/shard_map/reduce_scatter | solution.py:95
Sparse Core Ops, SparseCore 0:
  10.6 122.6 all-gather.1
  223.4 233.7 all-reduce.1
  461.3 242.1 reduce-scatter.1
where the time goes:
time: 715 us; the launch traced here: 712 us
  waiting for transfers between devices  485 us (68%)
  other arithmetic  93.1 us (13%)
  local copies, waits for them, and re-layouts  87.3 us (12%)
  matrix products  31.2 us (4%)
  between operations  14.5 us (2%)
    reduce_scatter x1, waiting for transfers between devices, body(): remote = lax.psum_scatter(spread, 'dom', scatter_dimension=0, tiled=True)  245 us
    psum x1, waiting for transfers between devices, body(): lax.psum(local_weight, ('dom', 'feat')) * (1.0 / math.sqrt(total_nodes))  136 us
    all_gather x1, waiting for transfers between devices, body(): source_table = lax.all_gather(sources, 'dom', axis=0, tiled=True)  104 us
    gather x8, local copies, waits for them, and re-layouts, forward_step(): picked = source_table[refs]  49.9 us
    scatter-add x8, other arithmetic, backward_step(): return (total.at[refs].add(product * mask[:, None, None]), None)  49.6 us
    scatter-add x8, other arithmetic, forward_step(): return (total.at[targets].add(product * mask[:, None, None]), None)  21.3 us
    dot_general x8, matrix products, forward_step(): jnp.einsum('tij,tjf->tif', tile_group, picked, preferred_element_type=jnp...  15.7 us
  transfers between devices with their start and end apart: 3, of which 3 were waited for; matrix products, arithmetic and copies ran while one was open for 17% of the time, Pallas kernels for 0%

commit v1 on v0

v1 whole, which is shorter than its diff:
```python
import functools
import math

import jax
import jax.numpy as jnp
from jax import lax
from jax.experimental import pallas as pl
from jax.experimental.pallas import tpu as pltpu
from jax.sharding import PartitionSpec as P

MESH = pl.DeviceIdType.MESH
VMEM = pltpu.VMEM
SMEM = pltpu.SMEM
DMA = pltpu.SemaphoreType.DMA
NY = 4
NZ = 8
TB = 128
SRC = 12
BLK = 8
SLOT = 2
NSLOT = NY * NZ * SLOT
NF = 8
W_SCALE = 1.0 / math.sqrt(BLK * TB * NY * NZ * NF)
UNROLL = 8


def _place():
    me = lax.axis_index("dom")
    return me // NZ, lax.rem(me, NZ)


def _at(y, z):
    return {"dom": lax.rem(y + NY, NY) * NZ + lax.rem(z + NZ, NZ)}


def _barrier(peers):
    sem = pltpu.get_barrier_semaphore()
    for peer in peers:
        pl.semaphore_signal(sem, inc=1, device_id=peer, device_id_type=MESH)
    pl.semaphore_wait(sem, len(peers))


GATHER_ORDER = (0, -1, 1, -2, 2, -3, 3, 4)


def gather_kernel(
    node, cached, need_v, need_s, gathered, peer_need,
    own, zp0, zm0, zp1, zm1, zp2, zm2, zfar, stage, pn_v, pn_s,
    in_sem, need_send, need_recv, pn_sem, z_send, z_recv, y_send, y_recv, keep_sem,
):
    y, z = _place()
    loads = [
        pltpu.make_async_copy(node, own.at[pl.ds(0, BLK)], in_sem.at[0]),
        pltpu.make_async_copy(cached, own.at[pl.ds(BLK, SRC - BLK)], in_sem.at[1]),
    ]
    for copy in loads:
        copy.start()
    _barrier([_at(y, z + 1), _at(y, z - 1)] + [_at(y + dy, z) for dy in range(1, NY)])
    asks = [
        pltpu.make_async_remote_copy(
            src_ref=need_v, dst_ref=pn_v.at[dy - 1],
            send_sem=need_send.at[dy - 1], recv_sem=need_recv.at[dy - 1],
            device_id=_at(y + dy, z), device_id_type=MESH,
        )
        for dy in range(1, NY)
    ]
    for copy in asks:
        copy.start()
    for copy in loads:
        copy.wait()
    half = SRC // 2
    first, second = pl.ds(0, half), pl.ds(half, half)

    def hop(src, dst, slot, dz):
        return pltpu.make_async_remote_copy(
            src_ref=src, dst_ref=dst, send_sem=z_send.at[slot], recv_sem=z_recv.at[slot],
            device_id=_at(y, z + dz), device_id_type=MESH,
        )

    def chain(stops, slot, dz, last):
        pairs = []
        for i in range(3):
            pairs.append(
                [
                    hop(stops[i].at[part], stops[i + 1].at[part], slot + 2 * i + n, dz)
                    for n, part in enumerate((first, second))
                ]
            )
        pairs.append([hop(stops[3].at[last], zfar.at[last], slot + 6, dz)])
        return pairs

    up = chain((own, zp0, zp1, zp2), 0, 1, first)
    down = chain((own, zm0, zm1, zm2), 7, -1, second)
    for n in range(2):
        up[0][n].start()
        down[0][n].start()
    for copy in asks:
        copy.wait()
    to_scalar = pltpu.make_async_copy(pn_v, pn_s, pn_sem)
    to_scalar.start()
    peer_need[...] = pn_v[...]
    to_scalar.wait()

    sends = []
    keeps = []

    def serve(buf, k):
        z0 = lax.rem(z + GATHER_ORDER[k] + NZ, NZ)
        mine = (y * NZ + z0) * SLOT
        for dy in range(1, NY):
            for s in range(SLOT):
                stage[dy, k, s] = buf[pn_s[NY - 1 - dy, 0, y * NZ + z0, s]]
            copy = pltpu.make_async_remote_copy(
                src_ref=stage.at[dy, k], dst_ref=gathered.at[pl.ds(mine, SLOT)],
                send_sem=y_send.at[dy - 1, k], recv_sem=y_recv.at[dy - 1, k],
                device_id=_at(y + dy, z), device_id_type=MESH,
            )
            copy.start()
            sends.append((dy, k, copy))
        for s in range(SLOT):
            stage[0, k, s] = buf[need_s[0, y * NZ + z0, s]]
        copy = pltpu.make_async_copy(
            stage.at[0, k], gathered.at[pl.ds(mine, SLOT)], keep_sem.at[k]
        )
        copy.start()
        keeps.append(copy)

    serve(own, 0)
    for step, (a, b) in enumerate(((zp0, zm0), (zp1, zm1), (zp2, zm2))):
        for n in range(2):
            for chained, forward in ((up, 0), (down, 1)):
                chained[step][n].wait_recv()
                if step < 2:
                    chained[step + 1][n].start()
                elif n == forward:
                    chained[3][0].start()
        serve(a, 1 + 2 * step)
        serve(b, 2 + 2 * step)
    up[3][0].wait_recv()
    down[3][0].wait_recv()
    serve(zfar, 7)
    for pairs in up + down:
        for copy in pairs:
            copy.wait_send()
    for copy in keeps:
        copy.wait()
    for dy, k, copy in sends:
        copy.wait_send()
        z0 = lax.rem(z + GATHER_ORDER[k] + NZ, NZ)
        theirs = (lax.rem(y + NY - dy, NY) * NZ + z0) * SLOT
        pltpu.make_async_remote_copy(
            src_ref=stage.at[dy, k], dst_ref=gathered.at[pl.ds(theirs, SLOT)],
            send_sem=y_send.at[dy - 1, k], recv_sem=y_recv.at[dy - 1, k],
            device_id=_at(y - dy, z), device_id_type=MESH,
        ).wait_recv()


def gather(node, cached, need):
    block = (SRC, TB, TB)
    return pl.pallas_call(
        gather_kernel,
        out_shape=(
            jax.ShapeDtypeStruct((NSLOT, TB, TB), jnp.bfloat16),
            jax.ShapeDtypeStruct((NY - 1, 1, NY * NZ, SLOT), jnp.int32),
        ),
        in_specs=[
            pl.BlockSpec(memory_space=pl.ANY),
            pl.BlockSpec(memory_space=pl.ANY),
            pl.BlockSpec(memory_space=VMEM),
            pl.BlockSpec(memory_space=SMEM),
        ],
        out_specs=(pl.BlockSpec(memory_space=pl.ANY), pl.BlockSpec(memory_space=VMEM)),
        scratch_shapes=[VMEM(block, jnp.bfloat16) for _ in range(8)]
        + [
            VMEM((NY, NZ, SLOT, TB, TB), jnp.bfloat16),
            VMEM((NY - 1, 1, NY * NZ, SLOT), jnp.int32),
            SMEM((NY - 1, 1, NY * NZ, SLOT), jnp.int32),
            DMA((2,)),
            DMA((NY - 1,)),
            DMA((NY - 1,)),
            DMA,
            DMA((14,)),
            DMA((14,)),
            DMA((NY - 1, NZ)),
            DMA((NY - 1, NZ)),
            DMA((NZ,)),
        ],
        compiler_params=pltpu.CompilerParams(
            collective_id=0, has_side_effects=True, vmem_limit_bytes=60 * 2**20
        ),
    )(node, cached, need, need)


def layer_kernel(
    row, col, count, tiles_h, node, cached, gathered, weights, grad_out,
    output, contrib, local_part, w_local,
    tiles, table, mixed_acc, grads_t, spread, tile_sem, table_sem,
):
    cap = tiles_h.shape[0]
    chunk = cap // 8
    table_loads = [
        pltpu.make_async_copy(node, table.at[pl.ds(0, BLK)], table_sem.at[0]),
        pltpu.make_async_copy(cached, table.at[pl.ds(BLK, SRC - BLK)], table_sem.at[1]),
        pltpu.make_async_copy(gathered, table.at[pl.ds(SRC, NSLOT)], table_sem.at[2]),
    ]
    for copy in table_loads:
        copy.start()

    def tile_load(i):
        span = pl.ds(i * chunk, chunk)
        return pltpu.make_async_copy(tiles_h.at[span], tiles.at[span], tile_sem.at[i])

    for i in range(8):
        tile_load(i).start()
    zero_src = SRC + NSLOT
    table[zero_src] = jnp.zeros((TB, TB), jnp.bfloat16)
    mixed_acc[...] = jnp.zeros_like(mixed_acc)
    used = count[0]
    for copy in table_loads:
        copy.wait()

    def steps(i):
        return jnp.clip((used - i * chunk + UNROLL - 1) // UNROLL, 0, chunk // UNROLL)

    def forward_chunk(i, _):
        tile_load(i).wait()

        def step(j, _):
            base = i * chunk + j * UNROLL
            products = []
            for u in range(UNROLL):
                t = base + u
                c = jnp.where(t < used, col[0, t], zero_src)
                products.append(jnp.dot(tiles[t], table[c], preferred_element_type=jnp.float32))
            for u in range(UNROLL):
                r = row[0, base + u]
                mixed_acc[r] += products[u]
            return 0

        return lax.fori_loop(0, steps(i), step, 0)

    lax.fori_loop(0, 8, forward_chunk, 0)

    w = weights[...]
    w_sum = jnp.zeros((TB, TB), jnp.float32)
    for r in range(BLK):
        mixed = mixed_acc[r].astype(jnp.bfloat16)
        pre = jnp.dot(mixed, w, preferred_element_type=jnp.float32)
        sig = jax.nn.sigmoid(pre)
        output[r] = (pre * sig).astype(jnp.bfloat16)
        act = (grad_out[r].astype(jnp.float32) * sig * (1.0 + pre * (1.0 - sig))).astype(jnp.bfloat16)
        grads_t[r] = lax.dot_general(
            w, act, (((1,), (1,)), ((), ())), preferred_element_type=jnp.float32
        ).astype(jnp.bfloat16)
        w_sum += lax.dot_general(
            mixed, act, (((0,), (0,)), ((), ())), preferred_element_type=jnp.float32
        )
    w_local[...] = w_sum
    grads_t[BLK] = jnp.zeros((TB, TB), jnp.bfloat16)
    spread[...] = jnp.zeros_like(spread)

    def backward_step(j, _):
        base = j * UNROLL
        products = []
        for u in range(UNROLL):
            t = base + u
            r = jnp.where(t < used, row[0, t], BLK)
            products.append(jnp.dot(grads_t[r], tiles[t], preferred_element_type=jnp.float32))
        for u in range(UNROLL):
            c = col[0, base + u]
            spread[c] += products[u]
        return 0

    lax.fori_loop(0, (used + UNROLL - 1) // UNROLL, backward_step, 0)
    for b in range(BLK):
        local_part[b] = spread[b]

    def cast(s, _):
        contrib[s] = spread[SRC + s].astype(jnp.bfloat16)
        return 0

    lax.fori_loop(0, NSLOT, cast, 0)


def layer(row, col, count, tiles, node, cached, gathered, weights, grad_out):
    cap = tiles.shape[0]
    flops = 4 * cap * TB**3
    vmem = pl.BlockSpec(memory_space=VMEM)
    smem = pl.BlockSpec(memory_space=SMEM)
    hbm = pl.BlockSpec(memory_space=pl.ANY)
    return pl.pallas_call(
        layer_kernel,
        out_shape=(
            jax.ShapeDtypeStruct((BLK, TB, TB), jnp.bfloat16),
            jax.ShapeDtypeStruct((NSLOT, TB, TB), jnp.bfloat16),
            jax.ShapeDtypeStruct((BLK, TB, TB), jnp.float32),
            jax.ShapeDtypeStruct((TB, TB), jnp.float32),
        ),
        in_specs=[smem, smem, smem, hbm, hbm, hbm, hbm, vmem, vmem],
        out_specs=(vmem, vmem, vmem, vmem),
        scratch_shapes=[
            VMEM((cap, TB, TB), jnp.bfloat16),
            VMEM((SRC + NSLOT + 1, TB, TB), jnp.bfloat16),
            VMEM((BLK, TB, TB), jnp.float32),
            VMEM((BLK + 1, TB, TB), jnp.bfloat16),
            VMEM((SRC + NSLOT, TB, TB), jnp.float32),
            DMA((8,)),
            DMA((3,)),
        ],
        compiler_params=pltpu.CompilerParams(vmem_limit_bytes=60 * 2**20),
        cost_estimate=pl.CostEstimate(
            flops=flops, bytes_accessed=16 * 2**20, transcendentals=BLK * TB * TB
        ),
    )(row, col, count, tiles, node, cached, gathered, weights, grad_out)


SCATTER_ORDER = (4, 3, -3, 2, -2, 1, -1, 0)


def scatter_kernel(
    contrib, local_part, w_local, need_s, peer_need, h_grad, w_grad,
    ybuf, ownc, sp4, sm4, sp3, sm3, sp2, sm2, sp1, sm1,
    rp3, rm3, rp2, rm2, rp1, rm1, rp0, rm0, h_sum,
    wf, wy, wz, own_sem, y_send, y_recv, z_send, z_recv,
    wf_send, wf_recv, wy_send, wy_recv, wz_send, wz_recv, wg_send, wg_recv,
):
    y, z = _place()
    f = lax.axis_index("feat")
    mine = pltpu.make_async_copy(contrib.at[pl.ds(y * NZ * SLOT, NZ * SLOT)], ownc, own_sem)
    mine.start()
    peers_f = [{"feat": lax.rem(f + df, NF)} for df in range(1, NF)]
    peers_y = [_at(y + dy, z) for dy in range(1, NY)]
    peers_z = [_at(y, z + dz) for dz in range(1, NZ)]
    _barrier(peers_f + peers_y + peers_z)
    piece = TB // NF

    def rows_of(i):
        return pl.ds(pl.multiple_of(i * piece, piece), piece)

    def tell(peers, srcs, dst, send_sem, recv_sem):
        copies = [
            pltpu.make_async_remote_copy(
                src_ref=src, dst_ref=dst, send_sem=send_sem.at[i], recv_sem=recv_sem.at[i],
                device_id=peer, device_id_type=MESH,
            )
            for i, (peer, src) in enumerate(zip(peers, srcs))
        ]
        for copy in copies:
            copy.start()
        return copies

    def finish(copies):
        for copy in copies:
            copy.wait()

    def summed(ref, n):
        acc = ref[0]
        for i in range(1, n):
            acc = acc + ref[i]
        return acc

    wf[f] = w_local[rows_of(f)]
    over_f = tell(
        peers_f, [w_local.at[rows_of(p["feat"])] for p in peers_f], wf.at[f], wf_send, wf_recv
    )
    sends = {}
    for k in range(NZ):
        z0 = lax.rem(z + SCATTER_ORDER[k] + NZ, NZ)
        for dy in range(1, NY):
            theirs = (lax.rem(y + dy, NY) * NZ + z0) * SLOT
            copy = pltpu.make_async_remote_copy(
                src_ref=contrib.at[pl.ds(theirs, SLOT)], dst_ref=ybuf.at[dy - 1, k],
                send_sem=y_send.at[dy - 1, k], recv_sem=y_recv.at[dy - 1, k],
                device_id=_at(y + dy, z), device_id_type=MESH,
            )
            copy.start()
            sends[dy, k] = copy
    mine.wait()
    half = BLK // 2
    rows = 32

    def total(k, lo, n, arrived, put):
        z0 = lax.rem(z + SCATTER_ORDER[k] + NZ, NZ)
        ids = [need_s[0, y * NZ + z0, s] for s in range(SLOT)]
        for dy in range(1, NY):
            ids += [peer_need[dy - 1, 0, y * NZ + z0, s] for s in range(SLOT)]

        def part(i, _):
            span = pl.ds(pl.multiple_of(i * rows, rows), rows)
            parts = [ownc[z0 * SLOT + s, span] for s in range(SLOT)]
            for dy in range(1, NY):
                parts += [ybuf[dy - 1, k, s, span] for s in range(SLOT)]
            parts = [p.astype(jnp.float32) for p in parts]
            for b in range(lo, lo + n):
                acc = arrived(b, span)
                for p, which in zip(parts, ids):
                    acc = acc + jnp.where(which == b, p, 0.0)
                put(b, span, acc)
            return 0

        lax.fori_loop(0, TB // rows, part, 0)

    def hop(src, dst, slot, dz):
        return pltpu.make_async_remote_copy(
            src_ref=src, dst_ref=dst, send_sem=z_send.at[slot], recv_sem=z_recv.at[slot],
            device_id=_at(y, z + dz), device_id_type=MESH,
        )

    def nothing(b, span):
        return jnp.zeros((rows, TB), jnp.float32)

    def into(ref, lo=0):
        def put(b, span, acc):
            ref[b - lo, span] = acc.astype(jnp.bfloat16)

        return put

    def arrive(k):
        for dy in range(1, NY):
            sends[dy, k].wait_recv()

    hops = []
    arrive(0)
    total(0, 0, half, nothing, into(sp4))
    hops.append(hop(sp4, rp3, 0, 1))
    hops[-1].start()
    total(0, half, half, nothing, into(sm4, half))
    hops.append(hop(sm4, rm3, 1, -1))
    hops[-1].start()

    def tail(ref, lo):
        def arrived(b, span):
            if lo <= b < lo + half:
                return ref[b - lo, span].astype(jnp.float32)
            return nothing(b, span)

        return arrived

    def whole(ref):
        return lambda b, span: ref[b, span].astype(jnp.float32)

    plan = (
        (rp3, sp3, rp2, 1), (rm3, sm3, rm2, -1),
        (rp2, sp2, rp1, 1), (rm2, sm2, rm1, -1),
        (rp1, sp1, rp0, 1), (rm1, sm1, rm0, -1),
    )
    for i, (got, out, there, dz) in enumerate(plan):
        k = i + 1
        if i == 1:
            finish(over_f)
            wy[y] = summed(wf, NF)
            over_y = tell(peers_y, [wy.at[y]] * (NY - 1), wy.at[y], wy_send, wy_recv)
        if i == 3:
            finish(over_y)
            wz[z] = summed(wy, NY)
            over_z = tell(peers_z, [wz.at[z]] * (NZ - 1), wz.at[z], wz_send, wz_recv)
        if i == 5:
            finish(over_z)
            w_grad[rows_of(f)] = summed(wz, NZ) * W_SCALE
            back = tell(
                peers_f, [w_grad.at[rows_of(f)]] * (NF - 1), w_grad.at[rows_of(f)], wg_send, wg_recv
            )
        arrive(k)
        hops[i].wait_recv()
        if i < 2:
            arrived = tail(got, 0 if dz == 1 else half)
        else:
            arrived = whole(got)
        total(k, 0, BLK, arrived, into(out))
        hops.append(hop(out, there, i + 2, dz))
        hops[-1].start()
    arrive(7)

    hops[6].wait_recv()
    hops[7].wait_recv()

    def last(b, span):
        return (
            local_part[b, span]
            + rp0[b, span].astype(jnp.float32)
            + rm0[b, span].astype(jnp.float32)
        )

    def put_last(b, span, acc):
        h_sum[b, span] = acc

    total(7, 0, BLK, last, put_last)
    for b in range(BLK):
        h_grad[b] = h_sum[b].T.astype(jnp.bfloat16)
    finish(back)
    for copy in hops:
        copy.wait_send()
    for copy in sends.values():
        copy.wait_send()


def scatter(contrib, local_part, w_local, need, peer_need):
    vmem = pl.BlockSpec(memory_space=VMEM)
    smem = pl.BlockSpec(memory_space=SMEM)
    bf = jnp.bfloat16
    blocks = [BLK // 2] * 2 + [BLK] * 6 + [BLK // 2] * 2 + [BLK] * 6
    return pl.pallas_call(
        scatter_kernel,
        out_shape=(
            jax.ShapeDtypeStruct((BLK, TB, TB), bf),
            jax.ShapeDtypeStruct((TB, TB), jnp.float32),
        ),
        in_specs=[pl.BlockSpec(memory_space=pl.ANY), vmem, vmem, smem, smem],
        out_specs=(vmem, vmem),
        scratch_shapes=[
            VMEM((NY - 1, NZ, SLOT, TB, TB), bf),
            VMEM((NZ * SLOT, TB, TB), bf),
        ]
        + [VMEM((n, TB, TB), bf) for n in blocks]
        + [VMEM((BLK, TB, TB), jnp.float32)]
        + [VMEM((n, TB // NF, TB), jnp.float32) for n in (NF, NY, NZ)]
        + [DMA, DMA((NY - 1, NZ)), DMA((NY - 1, NZ)), DMA((8,)), DMA((8,))]
        + [DMA((n - 1,)) for n in (NF, NF, NY, NY, NZ, NZ, NF, NF)],
        compiler_params=pltpu.CompilerParams(
            collective_id=1, has_side_effects=True, vmem_limit_bytes=60 * 2**20
        ),
    )(contrib, local_part, w_local, need, peer_need)


def body(node_feats, cached_feats, tile_values, tile_row, tile_col, tile_count, need_blocks, weights, grad_out):
    node = node_feats.reshape(BLK, TB, TB)
    cached = cached_feats.reshape(SRC - BLK, TB, TB)
    gathered, peer_need = gather(node, cached, need_blocks)
    output, contrib, local_part, w_local = layer(
        tile_row, tile_col, tile_count, tile_values, node, cached, gathered, weights,
        grad_out.reshape(BLK, TB, TB),
    )
    h_grad, w_grad = scatter(contrib, local_part, w_local, need_blocks, peer_need)
    return output.reshape(BLK * TB, TB), h_grad.reshape(BLK * TB, TB), w_grad


def solution(mesh):
    rows = P(("dom", "feat"), None)
    cubes = P(("dom", "feat"), None, None)
    in_specs = (rows, rows, cubes, rows, rows, P(("dom", "feat")), cubes, P(), rows)
    out_specs = (rows, rows, P())
    return jax.shard_map(body, mesh=mesh, in_specs=in_specs, out_specs=out_specs, check_vma=False)
```

time: 715 us -> 120 us (0.17)
  the two profiles are of different devices: /device:TPU:2 before, /device:TPU:1 now
where the time goes in v1:
time: 120 us
  Pallas kernels  114 us (95%)
  local copies, waits for them, and re-layouts  4.51 us (4%)
  between operations  1.3 us (1%)
    pallas_call x1, Pallas kernels, scatter(): pl.pallas_call(scatter_kernel, out_shape=(jax.ShapeDtypeStruct((BLK, TB,...  56.4 us
    pallas_call x1, Pallas kernels, gather(): pl.pallas_call(gather_kernel, out_shape=(jax.ShapeDtypeStruct((NSLOT, TB,...  46.7 us
    pallas_call x1, Pallas kernels, layer(): pl.pallas_call(layer_kernel, out_shape=(jax.ShapeDtypeStruct((BLK, TB, TB...  10.8 us
    unnamed x3, local copies, waits for them, and re-layouts  4.51 us

profile of v1, /device:TPU:1, one launch (start us, length us, event | category | flops | bytes accessed | tf_op | source)
XLA Modules:
  0.0 119.7 jit_solution(165541535383007282)
XLA Ops:
  1.3 1.4 %copy.12.need_v.need_s = s32[1,32,2]{2,1,0:T(8,128)} copy(s32[1,32,2]{1,2,0:T(2,128)} %param.15) | data formatting | bytes 512 | tf_op args[6]
  2.6 46.7 %shard_map.112 = (bf16[64,128,128]{2,1,0:T(8,128)(2,1)}, s32[3,1,32,2]{3,2,1,0:T(8,128)}) custom-call(bf16[8,128,128]{2,1,0:T(8,128)(2,1)} %bitcast.5, bf16[4,128,128]{2,1,0:T(8,128)(2,1)} %bitcast.7, s32[1,32,2]{2,1,0:T(8,128)} %copy.12.need_v.need_s, s32[1,32,2]{2,1,0:T(8,128)} %copy.12.need_v.need_s), custom_call_target="tpu_custom_call" | custom-call | tf_op jit(solution)/shard_map/pallas_call | solution.py:160
  49.3 10.8 %shard_map.113 = (bf16[8,128,128]{2,1,0:T(8,128)(2,1)}, bf16[64,128,128]{2,1,0:T(8,128)(2,1)}, f32[8,128,128]{2,1,0:T(8,128)}, f32[128,128]{1,0:T(8,128)}) custom-call(s32[1,256]{1,0:T(1,128)} %row.1, s32[1,256]{1,0:T(1,128)} %col.1, s32[1]{0:T(128)S(6)} %copy.17.count, bf16[256,128,128]{2,1,0:T(8,128)(2,1)} %tiles_h.1, bf16[8,128,128]{2,1,0:T(8,128)(2,1)} %bitcast.6, ...), custom_call_target="tpu_custom_call" | custom-call | flops 2147483648 | bytes 16777216 | tf_op jit(solution)/shard_map/pallas_call | solution.py:291
  60.2 56.4 %shard_map.114 = (bf16[8,128,128]{2,1,0:T(8,128)(2,1)}, f32[128,128]{1,0:T(8,128)}) custom-call(bf16[64,128,128]{2,1,0:T(8,128)(2,1)} %get-tuple-element.13.contrib, f32[8,128,128]{2,1,0:T(8,128)} %get-tuple-element.14.local_part, f32[128,128]{1,0:T(8,128)} %get-tuple-element.15.w_local, s32[1,32,2]{2,1,0:T(8,128)} %copy.12.need_v.need_s, ...), custom_call_target="tpu_custom_call" | custom-call | tf_op jit(solution)/shard_map/pallas_call | solution.py:502
  116.6 1.7 %copy.18 = bf16[1024,128]{1,0:T(8,128)(2,1)} copy(bf16[1024,128]{1,0:T(8,128)(2,1)} %bitcast.10) | data formatting | bytes 524288
  118.3 1.5 %copy.19 = f32[128,128]{1,0:T(8,128)} copy(f32[128,128]{1,0:T(8,128)} %get-tuple-element.24) | data formatting | bytes 131072

commit v2 on v1

--- a/solution.py
+++ b/solution.py
@@ -21,7 +21,8 @@
 NSLOT = NY * NZ * SLOT
 NF = 8
 W_SCALE = 1.0 / math.sqrt(BLK * TB * NY * NZ * NF)
-UNROLL = 8
+GROUP = 32
+CAST = 8
 
 
 def _place():
@@ -33,10 +34,12 @@
     return {"dom": lax.rem(y + NY, NY) * NZ + lax.rem(z + NZ, NZ)}
 
 
-def _barrier(peers):
+def _barrier(loads, peers):
     sem = pltpu.get_barrier_semaphore()
     for peer in peers:
         pl.semaphore_signal(sem, inc=1, device_id=peer, device_id_type=MESH)
+    for copy in loads:
+        copy.start()
     pl.semaphore_wait(sem, len(peers))
 
 
@@ -44,21 +47,20 @@
 
 
 def gather_kernel(
-    node, cached, need_v, need_s, gathered, peer_need,
-    own, zp0, zm0, zp1, zm1, zp2, zm2, zfar, stage, pn_v, pn_s,
-    in_sem, need_send, need_recv, pn_sem, z_send, z_recv, y_send, y_recv, keep_sem,
+    node, cached, need, gathered, peer_need,
+    own, need_s, zp0, zm0, zp1, zm1, zp2, zm2, zfar, stage, pn_v, pn_s,
+    in_sem, need_send, need_recv, pn_sem, out_sem, z_send, z_recv, y_send, y_recv, keep_sem,
 ):
     y, z = _place()
     loads = [
         pltpu.make_async_copy(node, own.at[pl.ds(0, BLK)], in_sem.at[0]),
         pltpu.make_async_copy(cached, own.at[pl.ds(BLK, SRC - BLK)], in_sem.at[1]),
+        pltpu.make_async_copy(need, need_s, in_sem.at[2]),
     ]
-    for copy in loads:
-        copy.start()
-    _barrier([_at(y, z + 1), _at(y, z - 1)] + [_at(y + dy, z) for dy in range(1, NY)])
+    _barrier(loads, [_at(y, z + 1), _at(y, z - 1)] + [_at(y + dy, z) for dy in range(1, NY)])
     asks = [
         pltpu.make_async_remote_copy(
-            src_ref=need_v, dst_ref=pn_v.at[dy - 1],
+            src_ref=need, dst_ref=pn_v.at[dy - 1],
             send_sem=need_send.at[dy - 1], recv_sem=need_recv.at[dy - 1],
             device_id=_at(y + dy, z), device_id_type=MESH,
         )
@@ -98,7 +100,8 @@
         copy.wait()
     to_scalar = pltpu.make_async_copy(pn_v, pn_s, pn_sem)
     to_scalar.start()
-    peer_need[...] = pn_v[...]
+    to_output = pltpu.make_async_copy(pn_v, peer_need, out_sem)
+    to_output.start()
     to_scalar.wait()
 
     sends = []
@@ -109,7 +112,7 @@
         mine = (y * NZ + z0) * SLOT
         for dy in range(1, NY):
             for s in range(SLOT):
-                stage[dy, k, s] = buf[pn_s[NY - 1 - dy, 0, y * NZ + z0, s]]
+                stage[dy, k, s] = buf[pn_s[NY - 1 - dy, 0, s, y * NZ + z0]]
             copy = pltpu.make_async_remote_copy(
                 src_ref=stage.at[dy, k], dst_ref=gathered.at[pl.ds(mine, SLOT)],
                 send_sem=y_send.at[dy - 1, k], recv_sem=y_recv.at[dy - 1, k],
@@ -118,7 +121,7 @@
             copy.start()
             sends.append((dy, k, copy))
         for s in range(SLOT):
-            stage[0, k, s] = buf[need_s[0, y * NZ + z0, s]]
+            stage[0, k, s] = buf[need_s[0, s, y * NZ + z0]]
         copy = pltpu.make_async_copy(
             stage.at[0, k], gathered.at[pl.ds(mine, SLOT)], keep_sem.at[k]
         )
@@ -142,6 +145,7 @@
     for pairs in up + down:
         for copy in pairs:
             copy.wait_send()
+    to_output.wait()
     for copy in keeps:
         copy.wait()
     for dy, k, copy in sends:
@@ -161,23 +165,20 @@
         gather_kernel,
         out_shape=(
             jax.ShapeDtypeStruct((NSLOT, TB, TB), jnp.bfloat16),
-            jax.ShapeDtypeStruct((NY - 1, 1, NY * NZ, SLOT), jnp.int32),
+            jax.ShapeDtypeStruct((NY - 1, 1, SLOT, NY * NZ), jnp.int32),
         ),
-        in_specs=[
-            pl.BlockSpec(memory_space=pl.ANY),
-            pl.BlockSpec(memory_space=pl.ANY),
-            pl.BlockSpec(memory_space=VMEM),
-            pl.BlockSpec(memory_space=SMEM),
-        ],
-        out_specs=(pl.BlockSpec(memory_space=pl.ANY), pl.BlockSpec(memory_space=VMEM)),
-        scratch_shapes=[VMEM(block, jnp.bfloat16) for _ in range(8)]
+        in_specs=[pl.BlockSpec(memory_space=pl.ANY)] * 3,
+        out_specs=(pl.BlockSpec(memory_space=pl.ANY),) * 2,
+        scratch_shapes=[VMEM(block, jnp.bfloat16), SMEM((1, SLOT, NY * NZ), jnp.int32)]
+        + [VMEM(block, jnp.bfloat16) for _ in range(7)]
         + [
             VMEM((NY, NZ, SLOT, TB, TB), jnp.bfloat16),
-            VMEM((NY - 1, 1, NY * NZ, SLOT), jnp.int32),
-            SMEM((NY - 1, 1, NY * NZ, SLOT), jnp.int32),
-            DMA((2,)),
+            VMEM((NY - 1, 1, SLOT, NY * NZ), jnp.int32),
+            SMEM((NY - 1, 1, SLOT, NY * NZ), jnp.int32),
+            DMA((3,)),
             DMA((NY - 1,)),
             DMA((NY - 1,)),
+            DMA,
             DMA,
             DMA((14,)),
             DMA((14,)),
@@ -188,58 +189,74 @@
         compiler_params=pltpu.CompilerParams(
             collective_id=0, has_side_effects=True, vmem_limit_bytes=60 * 2**20
         ),
-    )(node, cached, need, need)
+    )(node, cached, need)
 
 
 def layer_kernel(
-    row, col, count, tiles_h, node, cached, gathered, weights, grad_out,
-    output, contrib, local_part, w_local,
-    tiles, table, mixed_acc, grads_t, spread, tile_sem, table_sem,
+    row_h, col_h, count_h, tiles_h, node, cached, gathered, weights_h, grad_out_h,
+    output_h, contrib_h, local_h, w_local_h,
+    row, col, count, weights, grad_out, output, contrib, w_local,
+    tiles, table, mixed_acc, grads_t, spread, tile_sem, in_sem, out_sem, spread_sem,
 ):
-    cap = tiles_h.shape[0]
-    chunk = cap // 8
+    index_loads = [
+        pltpu.make_async_copy(src, dst, in_sem.at[i])
+        for i, (src, dst) in enumerate(((count_h, count), (row_h, row), (col_h, col)))
+    ]
     table_loads = [
-        pltpu.make_async_copy(node, table.at[pl.ds(0, BLK)], table_sem.at[0]),
-        pltpu.make_async_copy(cached, table.at[pl.ds(BLK, SRC - BLK)], table_sem.at[1]),
-        pltpu.make_async_copy(gathered, table.at[pl.ds(SRC, NSLOT)], table_sem.at[2]),
+        pltpu.make_async_copy(gathered, table.at[pl.ds(SRC, NSLOT)], in_sem.at[3]),
+        pltpu.make_async_copy(node, table.at[pl.ds(0, BLK)], in_sem.at[4]),
+        pltpu.make_async_copy(cached, table.at[pl.ds(BLK, SRC - BLK)], in_sem.at[5]),
     ]
-    for copy in table_loads:
+    dense_loads = [
+        pltpu.make_async_copy(weights_h, weights, in_sem.at[6]),
+        pltpu.make_async_copy(grad_out_h, grad_out, in_sem.at[7]),
+    ]
+    for copy in index_loads + table_loads:
         copy.start()
 
     def tile_load(i):
-        span = pl.ds(i * chunk, chunk)
+        span = pl.ds(i * GROUP, GROUP)
         return pltpu.make_async_copy(tiles_h.at[span], tiles.at[span], tile_sem.at[i])
 
-    for i in range(8):
+    index_loads[0].wait()
+    used = count[0]
+    groups = (used + GROUP - 1) // GROUP
+
+    def start_tiles(i, _):
         tile_load(i).start()
+        return 0
+
+    lax.fori_loop(0, groups, start_tiles, 0)
+    for copy in dense_loads:
+        copy.start()
     zero_src = SRC + NSLOT
     table[zero_src] = jnp.zeros((TB, TB), jnp.bfloat16)
+    grads_t[BLK] = jnp.zeros((TB, TB), jnp.bfloat16)
     mixed_acc[...] = jnp.zeros_like(mixed_acc)
-    used = count[0]
-    for copy in table_loads:
-        copy.wait()
-
-    def steps(i):
-        return jnp.clip((used - i * chunk + UNROLL - 1) // UNROLL, 0, chunk // UNROLL)
-
-    def forward_chunk(i, _):
+
+    def clear(c, _):
+        spread[c] = jnp.zeros((TB, TB), jnp.float32)
+        return 0
+
+    lax.fori_loop(0, SRC + NSLOT, clear, 0)
+    for copy in index_loads[1:] + table_loads:
+        copy.wait()
+
+    def forward_step(i, _):
         tile_load(i).wait()
-
-        def step(j, _):
-            base = i * chunk + j * UNROLL
-            products = []
-            for u in range(UNROLL):
-                t = base + u
-                c = jnp.where(t < used, col[0, t], zero_src)
-                products.append(jnp.dot(tiles[t], table[c], preferred_element_type=jnp.float32))
-            for u in range(UNROLL):
-                r = row[0, base + u]
-                mixed_acc[r] += products[u]
-            return 0
-
-        return lax.fori_loop(0, steps(i), step, 0)
-
-    lax.fori_loop(0, 8, forward_chunk, 0)
+        products = []
+        for u in range(GROUP):
+            t = i * GROUP + u
+            c = jnp.where(t < used, col[0, t], zero_src)
+            products.append(jnp.dot(tiles[t], table[c], preferred_element_type=jnp.float32))
+        for u in range(GROUP):
+            r = row[0, i * GROUP + u]
+            mixed_acc[r] += products[u]
+        return 0
+
+    lax.fori_loop(0, groups, forward_step, 0)
+    for copy in dense_loads:
+        copy.wait()
 
     w = weights[...]
     w_sum = jnp.zeros((TB, TB), jnp.float32)
@@ -256,56 +273,79 @@
             mixed, act, (((0,), (0,)), ((), ())), preferred_element_type=jnp.float32
         )
     w_local[...] = w_sum
-    grads_t[BLK] = jnp.zeros((TB, TB), jnp.bfloat16)
-    spread[...] = jnp.zeros_like(spread)
-
-    def backward_step(j, _):
-        base = j * UNROLL
+    stores = [
+        pltpu.make_async_copy(output, output_h, out_sem.at[0]),
+        pltpu.make_async_copy(w_local, w_local_h, out_sem.at[1]),
+    ]
+    for copy in stores:
+        copy.start()
+
+    def backward_step(i, _):
         products = []
-        for u in range(UNROLL):
-            t = base + u
+        for u in range(GROUP):
+            t = i * GROUP + u
             r = jnp.where(t < used, row[0, t], BLK)
             products.append(jnp.dot(grads_t[r], tiles[t], preferred_element_type=jnp.float32))
-        for u in range(UNROLL):
-            c = col[0, base + u]
+        for u in range(GROUP):
+            c = col[0, i * GROUP + u]
             spread[c] += products[u]
         return 0
 
-    lax.fori_loop(0, (used + UNROLL - 1) // UNROLL, backward_step, 0)
-    for b in range(BLK):
-        local_part[b] = spread[b]
-
-    def cast(s, _):
-        contrib[s] = spread[SRC + s].astype(jnp.bfloat16)
+    lax.fori_loop(0, groups, backward_step, 0)
+    stores.append(pltpu.make_async_copy(spread.at[pl.ds(0, BLK)], local_h, out_sem.at[2]))
+    stores[-1].start()
+
+    def store_part(i):
+        span = pl.ds(i * CAST, CAST)
+        return pltpu.make_async_copy(contrib.at[span], contrib_h.at[span], spread_sem.at[i])
+
+    def cast(i, _):
+        for u in range(CAST):
+            s = i * CAST + u
+            contrib[s] = spread[SRC + s].astype(jnp.bfloat16)
+        store_part(i).start()
         return 0
 
-    lax.fori_loop(0, NSLOT, cast, 0)
+    lax.fori_loop(0, NSLOT // CAST, cast, 0)
+    for i in range(NSLOT // CAST):
+        store_part(i).wait()
+    for copy in stores:
+        copy.wait()
 
 
 def layer(row, col, count, tiles, node, cached, gathered, weights, grad_out):
     cap = tiles.shape[0]
     flops = 4 * cap * TB**3
-    vmem = pl.BlockSpec(memory_space=VMEM)
-    smem = pl.BlockSpec(memory_space=SMEM)
     hbm = pl.BlockSpec(memory_space=pl.ANY)
+    bf, f32 = jnp.bfloat16, jnp.float32
     return pl.pallas_call(
         layer_kernel,
         out_shape=(
-            jax.ShapeDtypeStruct((BLK, TB, TB), jnp.bfloat16),
-            jax.ShapeDtypeStruct((NSLOT, TB, TB), jnp.bfloat16),
-            jax.ShapeDtypeStruct((BLK, TB, TB), jnp.float32),
-            jax.ShapeDtypeStruct((TB, TB), jnp.float32),
+            jax.ShapeDtypeStruct((BLK, TB, TB), bf),
+            jax.ShapeDtypeStruct((NSLOT, TB, TB), bf),
+            jax.ShapeDtypeStruct((BLK, TB, TB), f32),
+            jax.ShapeDtypeStruct((TB, TB), f32),
         ),
-        in_specs=[smem, smem, smem, hbm, hbm, hbm, hbm, vmem, vmem],
-        out_specs=(vmem, vmem, vmem, vmem),
+        in_specs=[hbm] * 9,
+        out_specs=(hbm,) * 4,
         scratch_shapes=[
-            VMEM((cap, TB, TB), jnp.bfloat16),
-            VMEM((SRC + NSLOT + 1, TB, TB), jnp.bfloat16),
-            VMEM((BLK, TB, TB), jnp.float32),
-            VMEM((BLK + 1, TB, TB), jnp.bfloat16),
-            VMEM((SRC + NSLOT, TB, TB), jnp.float32),
+            SMEM((1, cap), jnp.int32),
+            SMEM((1, cap), jnp.int32),
+            SMEM((1,), jnp.int32),
+            VMEM((TB, TB), bf),
+            VMEM((BLK, TB, TB), bf),
+            VMEM((BLK, TB, TB), bf),
+            VMEM((NSLOT, TB, TB), bf),
+            VMEM((TB, TB), f32),
+            VMEM((cap, TB, TB), bf),
+            VMEM((SRC + NSLOT + 1, TB, TB), bf),
+            VMEM((BLK, TB, TB), f32),
+            VMEM((BLK + 1, TB, TB), bf),
+            VMEM((SRC + NSLOT, TB, TB), f32),
+            DMA((cap // GROUP,)),
             DMA((8,)),
             DMA((3,)),
+            DMA((NSLOT // CAST,)),
         ],
         compiler_params=pltpu.CompilerParams(vmem_limit_bytes=60 * 2**20),
         cost_estimate=pl.CostEstimate(
@@ -318,20 +358,28 @@
 
 
 def scatter_kernel(
-    contrib, local_part, w_local, need_s, peer_need, h_grad, w_grad,
-    ybuf, ownc, sp4, sm4, sp3, sm3, sp2, sm2, sp1, sm1,
+    contrib, local_h, w_local_h, need_h, peer_need_h, h_grad_h, w_grad_h,
+    local_part, w_local, need_s, peer_need, h_grad, w_grad, ybuf, ownc, sp4, sm4, sp3, sm3, sp2, sm2, sp1, sm1,
     rp3, rm3, rp2, rm2, rp1, rm1, rp0, rm0, h_sum,
     wf, wy, wz, own_sem, y_send, y_recv, z_send, z_recv,
-    wf_send, wf_recv, wy_send, wy_recv, wz_send, wz_recv, wg_send, wg_recv,
+    load_sem, out_sem, wf_send, wf_recv, wy_send, wy_recv, wz_send, wz_recv, wg_send, wg_recv,
 ):
     y, z = _place()
     f = lax.axis_index("feat")
     mine = pltpu.make_async_copy(contrib.at[pl.ds(y * NZ * SLOT, NZ * SLOT)], ownc, own_sem)
-    mine.start()
+    loads = [
+        pltpu.make_async_copy(src, dst, load_sem.at[i])
+        for i, (src, dst) in enumerate(
+            (
+                (w_local_h, w_local), (local_h, local_part),
+                (need_h, need_s), (peer_need_h, peer_need),
+            )
+        )
+    ]
     peers_f = [{"feat": lax.rem(f + df, NF)} for df in range(1, NF)]
     peers_y = [_at(y + dy, z) for dy in range(1, NY)]
     peers_z = [_at(y, z + dz) for dz in range(1, NZ)]
-    _barrier(peers_f + peers_y + peers_z)
+    _barrier([mine] + loads, peers_f + peers_y + peers_z)
     piece = TB // NF
 
     def rows_of(i):
@@ -359,12 +407,14 @@
             acc = acc + ref[i]
         return acc
 
+    loads[0].wait()
     wf[f] = w_local[rows_of(f)]
     over_f = tell(
         peers_f, [w_local.at[rows_of(p["feat"])] for p in peers_f], wf.at[f], wf_send, wf_recv
     )
     sends = {}
-    for k in range(NZ):
+
+    def send(k):
         z0 = lax.rem(z + SCATTER_ORDER[k] + NZ, NZ)
         for dy in range(1, NY):
             theirs = (lax.rem(y + dy, NY) * NZ + z0) * SLOT
@@ -375,15 +425,23 @@
             )
             copy.start()
             sends[dy, k] = copy
-    mine.wait()
+
+    send(0)
+    finish(over_f)
+    wy[y] = summed(wf, NF)
+    over_y = tell(peers_y, [wy.at[y]] * (NY - 1), wy.at[y], wy_send, wy_recv)
+    send(1)
+    send(2)
+    for copy in [mine] + loads[1:]:
+        copy.wait()
     half = BLK // 2
     rows = 32
 
     def total(k, lo, n, arrived, put):
         z0 = lax.rem(z + SCATTER_ORDER[k] + NZ, NZ)
-        ids = [need_s[0, y * NZ + z0, s] for s in range(SLOT)]
+        ids = [need_s[0, s, y * NZ + z0] for s in range(SLOT)]
         for dy in range(1, NY):
-            ids += [peer_need[dy - 1, 0, y * NZ + z0, s] for s in range(SLOT)]
+            ids += [peer_need[dy - 1, 0, s, y * NZ + z0] for s in range(SLOT)]
 
         def part(i, _):
             span = pl.ds(pl.multiple_of(i * rows, rows), rows)
@@ -416,6 +474,8 @@
         return put
 
     def arrive(k):
+        if k + 3 < NZ:
+            send(k + 3)
         for dy in range(1, NY):
             sends[dy, k].wait_recv()
 
@@ -427,6 +487,9 @@
     total(0, half, half, nothing, into(sm4, half))
     hops.append(hop(sm4, rm3, 1, -1))
     hops[-1].start()
+    finish(over_y)
+    wz[z] = summed(wy, NY)
+    over_z = tell(peers_z, [wz.at[z]] * (NZ - 1), wz.at[z], wz_send, wz_recv)
 
     def tail(ref, lo):
         def arrived(b, span):
@@ -446,15 +509,7 @@
     )
     for i, (got, out, there, dz) in enumerate(plan):
         k = i + 1
-        if i == 1:
-            finish(over_f)
-            wy[y] = summed(wf, NF)
-            over_y = tell(peers_y, [wy.at[y]] * (NY - 1), wy.at[y], wy_send, wy_recv)
         if i == 3:
-            finish(over_y)
-            wz[z] = summed(wy, NY)
-            over_z = tell(peers_z, [wz.at[z]] * (NZ - 1), wz.at[z], wz_send, wz_recv)
-        if i == 5:
             finish(over_z)
             w_grad[rows_of(f)] = summed(wz, NZ) * W_SCALE
             back = tell(
@@ -485,9 +540,15 @@
         h_sum[b, span] = acc
 
     total(7, 0, BLK, last, put_last)
+    finish(back)
+    stores = [pltpu.make_async_copy(w_grad, w_grad_h, out_sem.at[BLK])]
+    stores[0].start()
     for b in range(BLK):
         h_grad[b] = h_sum[b].T.astype(jnp.bfloat16)
-    finish(back)
+        stores.append(pltpu.make_async_copy(h_grad.at[b], h_grad_h.at[b], out_sem.at[b]))
+        stores[-1].start()
+    for copy in stores:
+        copy.wait()
     for copy in hops:
         copy.wait_send()
     for copy in sends.values():
@@ -495,8 +556,7 @@
 
 
 def scatter(contrib, local_part, w_local, need, peer_need):
-    vmem = pl.BlockSpec(memory_space=VMEM)
-    smem = pl.BlockSpec(memory_space=SMEM)
+    hbm = pl.BlockSpec(memory_space=pl.ANY)
     bf = jnp.bfloat16
     blocks = [BLK // 2] * 2 + [BLK] * 6 + [BLK // 2] * 2 + [BLK] * 6
     return pl.pallas_call(
@@ -505,9 +565,15 @@
             jax.ShapeDtypeStruct((BLK, TB, TB), bf),
             jax.ShapeDtypeStruct((TB, TB), jnp.float32),
         ),
-        in_specs=[pl.BlockSpec(memory_space=pl.ANY), vmem, vmem, smem, smem],
-        out_specs=(vmem, vmem),
+        in_specs=[hbm] * 5,
+        out_specs=(hbm, hbm),
         scratch_shapes=[
+            VMEM((BLK, TB, TB), jnp.float32),
+            VMEM((TB, TB), jnp.float32),
+            SMEM((1, SLOT, NY * NZ), jnp.int32),
+            SMEM((NY - 1, 1, SLOT, NY * NZ), jnp.int32),
+            VMEM((BLK, TB, TB), bf),
+            VMEM((TB, TB), jnp.float32),
             VMEM((NY - 1, NZ, SLOT, TB, TB), bf),
             VMEM((NZ * SLOT, TB, TB), bf),
         ]
@@ -515,6 +581,7 @@
         + [VMEM((BLK, TB, TB), jnp.float32)]
         + [VMEM((n, TB // NF, TB), jnp.float32) for n in (NF, NY, NZ)]
         + [DMA, DMA((NY - 1, NZ)), DMA((NY - 1, NZ)), DMA((8,)), DMA((8,))]
+        + [DMA((4,)), DMA((BLK + 1,))]
         + [DMA((n - 1,)) for n in (NF, NF, NY, NY, NZ, NZ, NF, NF)],
         compiler_params=pltpu.CompilerParams(
             collective_id=1, has_side_effects=True, vmem_limit_bytes=60 * 2**20
@@ -525,12 +592,13 @@
 def body(node_feats, cached_feats, tile_values, tile_row, tile_col, tile_count, need_blocks, weights, grad_out):
     node = node_feats.reshape(BLK, TB, TB)
     cached = cached_feats.reshape(SRC - BLK, TB, TB)
-    gathered, peer_need = gather(node, cached, need_blocks)
+    need = jnp.swapaxes(need_blocks, 1, 2)
+    gathered, peer_need = gather(node, cached, need)
     output, contrib, local_part, w_local = layer(
         tile_row, tile_col, tile_count, tile_values, node, cached, gathered, weights,
         grad_out.reshape(BLK, TB, TB),
     )
-    h_grad, w_grad = scatter(contrib, local_part, w_local, need_blocks, peer_need)
+    h_grad, w_grad = scatter(contrib, local_part, w_local, need, peer_need)
     return output.reshape(BLK * TB, TB), h_grad.reshape(BLK * TB, TB), w_grad
 
 

time: 120 us -> 99.6 us (0.83)
  the two profiles are of different devices: /device:TPU:1 before, /device:TPU:2 now
where the time goes in v2:
time: 99.6 us; the launch traced here: 98.2 us
  Pallas kernels  93.8 us (94%)
  local copies, waits for them, and re-layouts  3.14 us (3%)
  between operations  1.3 us (1%)
    pallas_call x1, Pallas kernels, gather(): pl.pallas_call(gather_kernel, out_shape=(jax.ShapeDtypeStruct((NSLOT, TB,...  45.6 us
    pallas_call x1, Pallas kernels, scatter(): pl.pallas_call(scatter_kernel, out_shape=(jax.ShapeDtypeStruct((BLK, TB,...  42.3 us
    pallas_call x1, Pallas kernels, layer(): pl.pallas_call(layer_kernel, out_shape=(jax.ShapeDtypeStruct((BLK, TB, TB...  5.76 us
    unnamed x2, local copies, waits for them, and re-layouts  3.14 us

profile of v2, /device:TPU:2, one launch (start us, length us, event | category | flops | bytes accessed | tf_op | source)
XLA Modules:
  0.0 98.2 jit_solution(3016886362917408203)
XLA Ops:
  1.3 45.6 %shard_map.112 = (bf16[64,128,128]{2,1,0:T(8,128)(2,1)}, s32[3,1,2,32]{3,2,1,0:T(2,128)}) custom-call(bf16[8,128,128]{2,1,0:T(8,128)(2,1)} %bitcast.6, bf16[4,128,128]{2,1,0:T(8,128)(2,1)} %bitcast.8, s32[1,2,32]{2,1,0:T(2,128)} %bitcast.12), custom_call_target="tpu_custom_call" | custom-call | tf_op jit(solution)/shard_map/pallas_call | solution.py:164
  46.9 5.8 %shard_map.113 = (bf16[8,128,128]{2,1,0:T(8,128)(2,1)}, bf16[64,128,128]{2,1,0:T(8,128)(2,1)}, f32[8,128,128]{2,1,0:T(8,128)}, f32[128,128]{1,0:T(8,128)}) custom-call(s32[1,256]{1,0:T(1,128)} %row_h.1, s32[1,256]{1,0:T(1,128)} %col_h.1, s32[1]{0:T(128)S(6)} %copy.14.count_h, bf16[256,128,128]{2,1,0:T(8,128)(2,1)} %tiles_h.1, bf16[8,128,128]{2,1,0:T(8,128)(2,1)} %bitcast.7, ...), custom_call_target="tpu_custom_call" | custom-call | flops 2147483648 | bytes 16777216 | tf_op jit(solution)/shard_map/pallas_call | solution.py:321
  52.7 42.3 %shard_map.114 = (bf16[8,128,128]{2,1,0:T(8,128)(2,1)}, f32[128,128]{1,0:T(8,128)}) custom-call(bf16[64,128,128]{2,1,0:T(8,128)(2,1)} %get-tuple-element.13.contrib, f32[8,128,128]{2,1,0:T(8,128)} %get-tuple-element.14.local_h, f32[128,128]{1,0:T(8,128)} %get-tuple-element.15.w_local_h, s32[1,2,32]{2,1,0:T(2,128)} %bitcast.13, ...), custom_call_target="tpu_custom_call" | custom-call | tf_op jit(solution)/shard_map/pallas_call | solution.py:562
  95.1 1.7 %copy.15 = bf16[1024,128]{1,0:T(8,128)(2,1)} copy(bf16[1024,128]{1,0:T(8,128)(2,1)} %bitcast.11) | data formatting | bytes 524288
  96.7 1.5 %copy.16 = f32[128,128]{1,0:T(8,128)} copy(f32[128,128]{1,0:T(8,128)} %get-tuple-element.24) | data formatting | bytes 131072

commit v3 on v2

--- a/solution.py
+++ b/solution.py
@@ -20,6 +20,7 @@
 SLOT = 2
 NSLOT = NY * NZ * SLOT
 NF = 8
+PIECE = TB // NF
 W_SCALE = 1.0 / math.sqrt(BLK * TB * NY * NZ * NF)
 GROUP = 32
 CAST = 8
@@ -43,13 +44,16 @@
     pl.semaphore_wait(sem, len(peers))
 
 
-GATHER_ORDER = (0, -1, 1, -2, 2, -3, 3, 4)
+NEAR = (0, -1, 1, -2, 2)
+FAR = tuple((2, dy) for dy in (0, 1)) + tuple((-2, dy) for dy in (2, 3))
+FAR += tuple((dz, dy) for dy in range(NY) for dz in (1, -1))
 
 
 def gather_kernel(
     node, cached, need, gathered, peer_need,
-    own, need_s, zp0, zm0, zp1, zm1, zp2, zm2, zfar, stage, pn_v, pn_s,
-    in_sem, need_send, need_recv, pn_sem, out_sem, z_send, z_recv, y_send, y_recv, keep_sem,
+    own, need_s, zp0, zm0, zp1, zm1, stage, far_stage, pn_v, pn_s, fn_v, fn_s,
+    in_sem, need_send, need_recv, far_send, far_recv, pn_sem, fn_sem, out_sem,
+    z_send, z_recv, y_send, y_recv, keep_sem, f_send, f_recv,
 ):
     y, z = _place()
     loads = [
@@ -57,7 +61,33 @@
         pltpu.make_async_copy(cached, own.at[pl.ds(BLK, SRC - BLK)], in_sem.at[1]),
         pltpu.make_async_copy(need, need_s, in_sem.at[2]),
     ]
-    _barrier(loads, [_at(y, z + 1), _at(y, z - 1)] + [_at(y + dy, z) for dy in range(1, NY)])
+    offsets = [(dy, 0) for dy in range(1, NY)]
+    offsets += [(dy, dz) for dz in (1, -1) for dy in range(NY)]
+    offsets += [(dy, 2) for dy in (0, 1, 2)] + [(dy, -2) for dy in (0, 2, 3)]
+    _barrier(loads, [_at(y + dy, z + dz) for dy, dz in offsets])
+    for copy in loads[:2]:
+        copy.wait()
+    half = SRC // 2
+    parts = pl.ds(0, half), pl.ds(half, half)
+
+    def chain(stops, slot, dz):
+        return [
+            [
+                pltpu.make_async_remote_copy(
+                    src_ref=stops[i].at[part], dst_ref=stops[i + 1].at[part],
+                    send_sem=z_send.at[slot + 2 * i + n], recv_sem=z_recv.at[slot + 2 * i + n],
+                    device_id=_at(y, z + dz), device_id_type=MESH,
+                )
+                for n, part in enumerate(parts)
+            ]
+            for i in range(2)
+        ]
+
+    up = chain((own, zp0, zp1), 0, 1)
+    down = chain((own, zm0, zm1), 4, -1)
+    for n in range(2):
+        up[0][n].start()
+        down[0][n].start()
     asks = [
         pltpu.make_async_remote_copy(
             src_ref=need, dst_ref=pn_v.at[dy - 1],
@@ -66,36 +96,16 @@
         )
         for dy in range(1, NY)
     ]
-    for copy in asks:
+    far_asks = [
+        pltpu.make_async_remote_copy(
+            src_ref=need, dst_ref=fn_v.at[i], send_sem=far_send.at[i], recv_sem=far_recv.at[i],
+            device_id=_at(y - dy, z - dz), device_id_type=MESH,
+        )
+        for i, (dz, dy) in enumerate(FAR)
+    ]
+    for copy in asks + far_asks:
         copy.start()
-    for copy in loads:
-        copy.wait()
-    half = SRC // 2
-    first, second = pl.ds(0, half), pl.ds(half, half)
-
-    def hop(src, dst, slot, dz):
-        return pltpu.make_async_remote_copy(
-            src_ref=src, dst_ref=dst, send_sem=z_send.at[slot], recv_sem=z_recv.at[slot],
-            device_id=_at(y, z + dz), device_id_type=MESH,
-        )
-
-    def chain(stops, slot, dz, last):
-        pairs = []
-        for i in range(3):
-            pairs.append(
-                [
-                    hop(stops[i].at[part], stops[i + 1].at[part], slot + 2 * i + n, dz)
-                    for n, part in enumerate((first, second))
-                ]
-            )
-        pairs.append([hop(stops[3].at[last], zfar.at[last], slot + 6, dz)])
-        return pairs
-
-    up = chain((own, zp0, zp1, zp2), 0, 1, first)
-    down = chain((own, zm0, zm1, zm2), 7, -1, second)
-    for n in range(2):
-        up[0][n].start()
-        down[0][n].start()
+    loads[2].wait()
     for copy in asks:
         copy.wait()
     to_scalar = pltpu.make_async_copy(pn_v, pn_s, pn_sem)
@@ -104,17 +114,19 @@
     to_output.start()
     to_scalar.wait()
 
+    def slots(y0, z0):
+        return pl.ds((lax.rem(y0 + NY, NY) * NZ + lax.rem(z0 + NZ, NZ)) * SLOT, SLOT)
+
     sends = []
     keeps = []
 
     def serve(buf, k):
-        z0 = lax.rem(z + GATHER_ORDER[k] + NZ, NZ)
-        mine = (y * NZ + z0) * SLOT
+        z0 = lax.rem(z + NEAR[k] + NZ, NZ)
         for dy in range(1, NY):
             for s in range(SLOT):
                 stage[dy, k, s] = buf[pn_s[NY - 1 - dy, 0, s, y * NZ + z0]]
             copy = pltpu.make_async_remote_copy(
-                src_ref=stage.at[dy, k], dst_ref=gathered.at[pl.ds(mine, SLOT)],
+                src_ref=stage.at[dy, k], dst_ref=gathered.at[slots(y, z0)],
                 send_sem=y_send.at[dy - 1, k], recv_sem=y_recv.at[dy - 1, k],
                 device_id=_at(y + dy, z), device_id_type=MESH,
             )
@@ -122,26 +134,41 @@
             sends.append((dy, k, copy))
         for s in range(SLOT):
             stage[0, k, s] = buf[need_s[0, s, y * NZ + z0]]
-        copy = pltpu.make_async_copy(
-            stage.at[0, k], gathered.at[pl.ds(mine, SLOT)], keep_sem.at[k]
-        )
+        copy = pltpu.make_async_copy(stage.at[0, k], gathered.at[slots(y, z0)], keep_sem.at[k])
         copy.start()
         keeps.append(copy)
 
     serve(own, 0)
-    for step, (a, b) in enumerate(((zp0, zm0), (zp1, zm1), (zp2, zm2))):
-        for n in range(2):
-            for chained, forward in ((up, 0), (down, 1)):
-                chained[step][n].wait_recv()
-                if step < 2:
-                    chained[step + 1][n].start()
-                elif n == forward:
-                    chained[3][0].start()
-        serve(a, 1 + 2 * step)
-        serve(b, 2 + 2 * step)
-    up[3][0].wait_recv()
-    down[3][0].wait_recv()
-    serve(zfar, 7)
+    for n in range(2):
+        up[0][n].wait_recv()
+        up[1][n].start()
+        down[0][n].wait_recv()
+        down[1][n].start()
+    serve(zp0, 1)
+    serve(zm0, 2)
+    for copy in far_asks:
+        copy.wait()
+    to_scalar = pltpu.make_async_copy(fn_v, fn_s, fn_sem)
+    to_scalar.start()
+    to_scalar.wait()
+    for n in range(2):
+        up[1][n].wait_recv()
+        down[1][n].wait_recv()
+    far_sends = []
+    for i, (dz, dy) in enumerate(FAR):
+        buf, back = (zp1, -2) if dz > 0 else (zm1, 2)
+        z0 = lax.rem(z + back + NZ, NZ)
+        for s in range(SLOT):
+            far_stage[i, s] = buf[fn_s[i, 0, s, y * NZ + z0]]
+        copy = pltpu.make_async_remote_copy(
+            src_ref=far_stage.at[i], dst_ref=gathered.at[slots(y, z0)],
+            send_sem=f_send.at[i], recv_sem=f_recv.at[i],
+            device_id=_at(y + dy, z + dz), device_id_type=MESH,
+        )
+        copy.start()
+        far_sends.append(copy)
+    serve(zp1, 3)
+    serve(zm1, 4)
     for pairs in up + down:
         for copy in pairs:
             copy.wait_send()
@@ -150,12 +177,18 @@
         copy.wait()
     for dy, k, copy in sends:
         copy.wait_send()
-        z0 = lax.rem(z + GATHER_ORDER[k] + NZ, NZ)
-        theirs = (lax.rem(y + NY - dy, NY) * NZ + z0) * SLOT
         pltpu.make_async_remote_copy(
-            src_ref=stage.at[dy, k], dst_ref=gathered.at[pl.ds(theirs, SLOT)],
+            src_ref=stage.at[dy, k], dst_ref=gathered.at[slots(y - dy, z + NEAR[k])],
             send_sem=y_send.at[dy - 1, k], recv_sem=y_recv.at[dy - 1, k],
             device_id=_at(y - dy, z), device_id_type=MESH,
+        ).wait_recv()
+    for i, (dz, dy) in enumerate(FAR):
+        far_sends[i].wait_send()
+        back = -2 if dz > 0 else 2
+        pltpu.make_async_remote_copy(
+            src_ref=far_stage.at[i], dst_ref=gathered.at[slots(y - dy, z - dz + back)],
+            send_sem=f_send.at[i], recv_sem=f_recv.at[i],
+            device_id=_at(y - dy, z - dz), device_id_type=MESH,
         ).wait_recv()
 
 
@@ -169,22 +202,34 @@
         ),
         in_specs=[pl.BlockSpec(memory_space=pl.ANY)] * 3,
         out_specs=(pl.BlockSpec(memory_space=pl.ANY),) * 2,
-        scratch_shapes=[VMEM(block, jnp.bfloat16), SMEM((1, SLOT, NY * NZ), jnp.int32)]
-        + [VMEM(block, jnp.bfloat16) for _ in range(7)]
-        + [
-            VMEM((NY, NZ, SLOT, TB, TB), jnp.bfloat16),
+        scratch_shapes=[
+            VMEM(block, jnp.bfloat16),
+            SMEM((1, SLOT, NY * NZ), jnp.int32),
+            VMEM(block, jnp.bfloat16),
+            VMEM(block, jnp.bfloat16),
+            VMEM(block, jnp.bfloat16),
+            VMEM(block, jnp.bfloat16),
+            VMEM((NY, len(NEAR), SLOT, TB, TB), jnp.bfloat16),
+            VMEM((len(FAR), SLOT, TB, TB), jnp.bfloat16),
             VMEM((NY - 1, 1, SLOT, NY * NZ), jnp.int32),
             SMEM((NY - 1, 1, SLOT, NY * NZ), jnp.int32),
+            VMEM((len(FAR), 1, SLOT, NY * NZ), jnp.int32),
+            SMEM((len(FAR), 1, SLOT, NY * NZ), jnp.int32),
             DMA((3,)),
             DMA((NY - 1,)),
             DMA((NY - 1,)),
+            DMA((len(FAR),)),
+            DMA((len(FAR),)),
             DMA,
             DMA,
-            DMA((14,)),
-            DMA((14,)),
-            DMA((NY - 1, NZ)),
-            DMA((NY - 1, NZ)),
-            DMA((NZ,)),
+            DMA,
+            DMA((8,)),
+            DMA((8,)),
+            DMA((NY - 1, len(NEAR))),
+            DMA((NY - 1, len(NEAR))),
+            DMA((len(NEAR),)),
+            DMA((len(FAR),)),
+            DMA((len(FAR),)),
         ],
         compiler_params=pltpu.CompilerParams(
             collective_id=0, has_side_effects=True, vmem_limit_bytes=60 * 2**20
@@ -380,7 +425,7 @@
     peers_y = [_at(y + dy, z) for dy in range(1, NY)]
     peers_z = [_at(y, z + dz) for dz in range(1, NZ)]
     _barrier([mine] + loads, peers_f + peers_y + peers_z)
-    piece = TB // NF
+    piece = PIECE
 
     def rows_of(i):
         return pl.ds(pl.multiple_of(i * piece, piece), piece)
@@ -426,12 +471,8 @@
             copy.start()
             sends[dy, k] = copy
 
-    send(0)
-    finish(over_f)
-    wy[y] = summed(wf, NF)
-    over_y = tell(peers_y, [wy.at[y]] * (NY - 1), wy.at[y], wy_send, wy_recv)
-    send(1)
-    send(2)
+    for k in range(NZ):
+        send(k)
     for copy in [mine] + loads[1:]:
         copy.wait()
     half = BLK // 2
@@ -474,60 +515,61 @@
         return put
 
     def arrive(k):
-        if k + 3 < NZ:
-            send(k + 3)
         for dy in range(1, NY):
             sends[dy, k].wait_recv()
 
+    def half_of(ref, n):
+        return ref.at[pl.ds(n * half, half)]
+
     hops = []
+
+    def forward(src, dst, dz):
+        hops.append(hop(src, dst, len(hops), dz))
+        hops[-1].start()
+        return hops[-1]
+
+    finish(over_f)
+    wz[z] = summed(wf, NF)
+    over_z = tell(peers_z, [wz.at[z]] * (NZ - 1), wz.at[z], wz_send, wz_recv)
     arrive(0)
     total(0, 0, half, nothing, into(sp4))
-    hops.append(hop(sp4, rp3, 0, 1))
-    hops[-1].start()
+    coming_up = [forward(sp4, rp3, 1), None]
     total(0, half, half, nothing, into(sm4, half))
-    hops.append(hop(sm4, rm3, 1, -1))
-    hops[-1].start()
-    finish(over_y)
-    wz[z] = summed(wy, NY)
-    over_z = tell(peers_z, [wz.at[z]] * (NZ - 1), wz.at[z], wz_send, wz_recv)
-
-    def tail(ref, lo):
-        def arrived(b, span):
-            if lo <= b < lo + half:
-                return ref[b - lo, span].astype(jnp.float32)
-            return nothing(b, span)
-
-        return arrived
+    coming_down = [None, forward(sm4, rm3, -1)]
 
     def whole(ref):
         return lambda b, span: ref[b, span].astype(jnp.float32)
 
-    plan = (
-        (rp3, sp3, rp2, 1), (rm3, sm3, rm2, -1),
-        (rp2, sp2, rp1, 1), (rm2, sm2, rm1, -1),
-        (rp1, sp1, rp0, 1), (rm1, sm1, rm0, -1),
+    def far(ref, lo):
+        return lambda b, span: ref[b - lo, span].astype(jnp.float32)
+
+    def step(k, coming, got, out, there, dz):
+        arrive(k)
+        leaving = [None, None]
+        for n in (1, 0) if dz == 1 else (0, 1):
+            arrived = nothing
+            if coming[n] is not None:
+                coming[n].wait_recv()
+                arrived = whole(got) if k > 2 else far(got, n * half)
+            total(k, n * half, half, arrived, into(out))
+            leaving[n] = forward(half_of(out, n), half_of(there, n), dz)
+        return leaving
+
+    coming_up = step(1, coming_up, rp3, sp3, rp2, 1)
+    coming_down = step(2, coming_down, rm3, sm3, rm2, -1)
+    finish(over_z)
+    wy[y] = summed(wz, NZ)
+    over_y = tell(peers_y, [wy.at[y]] * (NY - 1), wy.at[y], wy_send, wy_recv)
+    coming_up = step(3, coming_up, rp2, sp2, rp1, 1)
+    coming_down = step(4, coming_down, rm2, sm2, rm1, -1)
+    coming_up = step(5, coming_up, rp1, sp1, rp0, 1)
+    finish(over_y)
+    w_grad[rows_of(f)] = summed(wy, NY) * W_SCALE
+    back = tell(
+        peers_f, [w_grad.at[rows_of(f)]] * (NF - 1), w_grad.at[rows_of(f)], wg_send, wg_recv
     )
-    for i, (got, out, there, dz) in enumerate(plan):
-        k = i + 1
-        if i == 3:
-            finish(over_z)
-            w_grad[rows_of(f)] = summed(wz, NZ) * W_SCALE
-            back = tell(
-                peers_f, [w_grad.at[rows_of(f)]] * (NF - 1), w_grad.at[rows_of(f)], wg_send, wg_recv
-            )
-        arrive(k)
-        hops[i].wait_recv()
-        if i < 2:
-            arrived = tail(got, 0 if dz == 1 else half)
-        else:
-            arrived = whole(got)
-        total(k, 0, BLK, arrived, into(out))
-        hops.append(hop(out, there, i + 2, dz))
-        hops[-1].start()
+    coming_down = step(6, coming_down, rm1, sm1, rm0, -1)
     arrive(7)
-
-    hops[6].wait_recv()
-    hops[7].wait_recv()
 
     def last(b, span):
         return (
@@ -539,20 +581,26 @@
     def put_last(b, span, acc):
         h_sum[b, span] = acc
 
-    total(7, 0, BLK, last, put_last)
-    finish(back)
-    stores = [pltpu.make_async_copy(w_grad, w_grad_h, out_sem.at[BLK])]
-    stores[0].start()
-    for b in range(BLK):
-        h_grad[b] = h_sum[b].T.astype(jnp.bfloat16)
-        stores.append(pltpu.make_async_copy(h_grad.at[b], h_grad_h.at[b], out_sem.at[b]))
+    stores = []
+    for copy in coming_up + coming_down:
+        copy.wait_recv()
+    for n in range(2):
+        total(7, n * half, half, last, put_last)
+        for b in range(n * half, n * half + half):
+            h_grad[b] = h_sum[b].T.astype(jnp.bfloat16)
+        stores.append(
+            pltpu.make_async_copy(half_of(h_grad, n), half_of(h_grad_h, n), out_sem.at[n])
+        )
         stores[-1].start()
-    for copy in stores:
-        copy.wait()
     for copy in hops:
         copy.wait_send()
     for copy in sends.values():
         copy.wait_send()
+    finish(back)
+    stores.append(pltpu.make_async_copy(w_grad, w_grad_h, out_sem.at[2]))
+    stores[-1].start()
+    for copy in stores:
+        copy.wait()
 
 
 def scatter(contrib, local_part, w_local, need, peer_need):
@@ -579,9 +627,9 @@
         ]
         + [VMEM((n, TB, TB), bf) for n in blocks]
         + [VMEM((BLK, TB, TB), jnp.float32)]
-        + [VMEM((n, TB // NF, TB), jnp.float32) for n in (NF, NY, NZ)]
-        + [DMA, DMA((NY - 1, NZ)), DMA((NY - 1, NZ)), DMA((8,)), DMA((8,))]
-        + [DMA((4,)), DMA((BLK + 1,))]
+        + [VMEM((n, PIECE, TB), jnp.float32) for n in (NF, NY, NZ)]
+        + [DMA, DMA((NY - 1, NZ)), DMA((NY - 1, NZ)), DMA((14,)), DMA((14,))]
+        + [DMA((4,)), DMA((3,))]
         + [DMA((n - 1,)) for n in (NF, NF, NY, NY, NZ, NZ, NF, NF)],
         compiler_params=pltpu.CompilerParams(
             collective_id=1, has_side_effects=True, vmem_limit_bytes=60 * 2**20

time: 99.6 us -> 97.6 us (0.980)
  Pallas kernels: 93.8 us -> 91.3 us
    pallas_call x1, Pallas kernels: 42.3 us -> 38.6 us  [scatter(): pl.pallas_call(scatter_kernel, out_shape=(jax.ShapeDtypeStruct((BLK, TB,...]
    pallas_call x1, Pallas kernels: 5.76 us -> 8.62 us  [layer(): pl.pallas_call(layer_kernel, out_shape=(jax.ShapeDtypeStruct((BLK, TB, TB...]
    pallas_call x1, Pallas kernels: 45.6 us -> 44.1 us  [gather(): pl.pallas_call(gather_kernel, out_shape=(jax.ShapeDtypeStruct((NSLOT, TB,...]
where the time goes in v3:
time: 97.6 us; the launch traced here: 95.7 us
  Pallas kernels  91.3 us (94%)
  local copies, waits for them, and re-layouts  3.14 us (3%)
  between operations  1.3 us (1%)
    pallas_call x1, Pallas kernels, gather(): pl.pallas_call(gather_kernel, out_shape=(jax.ShapeDtypeStruct((NSLOT, TB,...  44.1 us
    pallas_call x1, Pallas kernels, scatter(): pl.pallas_call(scatter_kernel, out_shape=(jax.ShapeDtypeStruct((BLK, TB,...  38.6 us
    pallas_call x1, Pallas kernels, layer(): pl.pallas_call(layer_kernel, out_shape=(jax.ShapeDtypeStruct((BLK, TB, TB...  8.62 us
    unnamed x2, local copies, waits for them, and re-layouts  3.14 us

profile of v3, /device:TPU:2, one launch (start us, length us, event | category | flops | bytes accessed | tf_op | source)
XLA Modules:
  0.0 95.7 jit_solution(9884090749108643215)
XLA Ops:
  1.3 44.1 %shard_map.112 = (bf16[64,128,128]{2,1,0:T(8,128)(2,1)}, s32[3,1,2,32]{3,2,1,0:T(2,128)}) custom-call(bf16[8,128,128]{2,1,0:T(8,128)(2,1)} %bitcast.6, bf16[4,128,128]{2,1,0:T(8,128)(2,1)} %bitcast.8, s32[1,2,32]{2,1,0:T(2,128)} %bitcast.12), custom_call_target="tpu_custom_call" | custom-call | tf_op jit(solution)/shard_map/pallas_call | solution.py:197
  45.4 8.6 %shard_map.113 = (bf16[8,128,128]{2,1,0:T(8,128)(2,1)}, bf16[64,128,128]{2,1,0:T(8,128)(2,1)}, f32[8,128,128]{2,1,0:T(8,128)}, f32[128,128]{1,0:T(8,128)}) custom-call(s32[1,256]{1,0:T(1,128)} %row_h.1, s32[1,256]{1,0:T(1,128)} %col_h.1, s32[1]{0:T(128)S(6)} %copy.14.count_h, bf16[256,128,128]{2,1,0:T(8,128)(2,1)} %tiles_h.1, bf16[8,128,128]{2,1,0:T(8,128)(2,1)} %bitcast.7, ...), custom_call_target="tpu_custom_call" | custom-call | flops 2147483648 | bytes 16777216 | tf_op jit(solution)/shard_map/pallas_call | solution.py:366
  54.0 38.6 %shard_map.114 = (bf16[8,128,128]{2,1,0:T(8,128)(2,1)}, f32[128,128]{1,0:T(8,128)}) custom-call(bf16[64,128,128]{2,1,0:T(8,128)(2,1)} %get-tuple-element.13.contrib, f32[8,128,128]{2,1,0:T(8,128)} %get-tuple-element.14.local_h, f32[128,128]{1,0:T(8,128)} %get-tuple-element.15.w_local_h, s32[1,2,32]{2,1,0:T(2,128)} %bitcast.13, ...), custom_call_target="tpu_custom_call" | custom-call | tf_op jit(solution)/shard_map/pallas_call | solution.py:610
  92.6 1.7 %copy.15 = bf16[1024,128]{1,0:T(8,128)(2,1)} copy(bf16[1024,128]{1,0:T(8,128)(2,1)} %bitcast.11) | data formatting | bytes 524288
  94.2 1.5 %copy.16 = f32[128,128]{1,0:T(8,128)} copy(f32[128,128]{1,0:T(8,128)} %get-tuple-element.24) | data formatting | bytes 131072

commit v4 on v3

--- a/solution.py
+++ b/solution.py
@@ -571,23 +571,20 @@
     coming_down = step(6, coming_down, rm1, sm1, rm0, -1)
     arrive(7)
 
-    def last(b, span):
-        return (
-            local_part[b, span]
-            + rp0[b, span].astype(jnp.float32)
-            + rm0[b, span].astype(jnp.float32)
-        )
+    def local(b, span):
+        return local_part[b, span]
 
     def put_last(b, span, acc):
         h_sum[b, span] = acc
 
     stores = []
-    for copy in coming_up + coming_down:
-        copy.wait_recv()
+    total(7, 0, BLK, local, put_last)
     for n in range(2):
-        total(7, n * half, half, last, put_last)
+        coming_up[n].wait_recv()
+        coming_down[n].wait_recv()
         for b in range(n * half, n * half + half):
-            h_grad[b] = h_sum[b].T.astype(jnp.bfloat16)
+            whole_sum = h_sum[b] + rp0[b].astype(jnp.float32) + rm0[b].astype(jnp.float32)
+            h_grad[b] = whole_sum.T.astype(jnp.bfloat16)
         stores.append(
             pltpu.make_async_copy(half_of(h_grad, n), half_of(h_grad_h, n), out_sem.at[n])
         )
@@ -610,11 +607,11 @@
     return pl.pallas_call(
         scatter_kernel,
         out_shape=(
-            jax.ShapeDtypeStruct((BLK, TB, TB), bf),
-            jax.ShapeDtypeStruct((TB, TB), jnp.float32),
+            VMEM((BLK, TB, TB), bf),
+            VMEM((TB, TB), jnp.float32),
         ),
         in_specs=[hbm] * 5,
-        out_specs=(hbm, hbm),
+        out_specs=(pl.BlockSpec(memory_space=VMEM),) * 2,
         scratch_shapes=[
             VMEM((BLK, TB, TB), jnp.float32),
             VMEM((TB, TB), jnp.float32),
@@ -632,7 +629,7 @@
         + [DMA((4,)), DMA((3,))]
         + [DMA((n - 1,)) for n in (NF, NF, NY, NY, NZ, NZ, NF, NF)],
         compiler_params=pltpu.CompilerParams(
-            collective_id=1, has_side_effects=True, vmem_limit_bytes=60 * 2**20
+            collective_id=1, has_side_effects=True, vmem_limit_bytes=56 * 2**20
         ),
     )(contrib, local_part, w_local, need, peer_need)
 

time: 97.6 us -> 95.2 us (0.975); the launches traced: 95.7 us -> 95.1 us
  local copies, waits for them, and re-layouts: 3.14 us -> 1.33 us
  Pallas kernels: 91.3 us -> 92.4 us
    pallas_call x1, Pallas kernels: 38.6 us -> 40.7 us  [scatter(): pl.pallas_call(scatter_kernel, out_shape=(VMEM((BLK, TB, TB), bf), VMEM((...]
    unnamed x2, local copies, waits for them, and re-layouts: 3.14 us -> 1.33 us
where the time goes in v4:
time: 95.2 us; the launch traced here: 95.1 us
  Pallas kernels  92.4 us (97%)
  local copies, waits for them, and re-layouts  1.33 us (1%)
  between operations  1.3 us (1%)
    pallas_call x1, Pallas kernels, gather(): pl.pallas_call(gather_kernel, out_shape=(jax.ShapeDtypeStruct((NSLOT, TB,...  44.1 us
    pallas_call x1, Pallas kernels, scatter(): pl.pallas_call(scatter_kernel, out_shape=(VMEM((BLK, TB, TB), bf), VMEM((...  40.7 us
    pallas_call x1, Pallas kernels, layer(): pl.pallas_call(layer_kernel, out_shape=(jax.ShapeDtypeStruct((BLK, TB, TB...  7.64 us

profile of v4, /device:TPU:2, one launch (start us, length us, event | category | flops | bytes accessed | tf_op | source)
XLA Modules:
  0.0 95.1 jit_solution(14280116371757931688)
XLA Ops:
  1.3 44.1 %shard_map.112 = (bf16[64,128,128]{2,1,0:T(8,128)(2,1)}, s32[3,1,2,32]{3,2,1,0:T(2,128)}) custom-call(bf16[8,128,128]{2,1,0:T(8,128)(2,1)} %bitcast.7, bf16[4,128,128]{2,1,0:T(8,128)(2,1)} %bitcast.9, s32[1,2,32]{2,1,0:T(2,128)} %bitcast.12), custom_call_target="tpu_custom_call" | custom-call | tf_op jit(solution)/shard_map/pallas_call | solution.py:197
  45.4 7.6 %shard_map.113 = (bf16[8,128,128]{2,1,0:T(8,128)(2,1)}, bf16[64,128,128]{2,1,0:T(8,128)(2,1)}, f32[8,128,128]{2,1,0:T(8,128)}, f32[128,128]{1,0:T(8,128)}) custom-call(s32[1,256]{1,0:T(1,128)} %row_h.1, s32[1,256]{1,0:T(1,128)} %col_h.1, s32[1]{0:T(128)S(6)} %copy.16.count_h, bf16[256,128,128]{2,1,0:T(8,128)(2,1)} %tiles_h.1, bf16[8,128,128]{2,1,0:T(8,128)(2,1)} %bitcast.8, ...), custom_call_target="tpu_custom_call" | custom-call | flops 2147483648 | bytes 16777216 | tf_op jit(solution)/shard_map/pallas_call | solution.py:366
  53.0 40.7 %shard_map.114 = (bf16[8,128,128]{2,1,0:T(8,128)(2,1)S(1)}, f32[128,128]{1,0:T(8,128)S(1)}) custom-call(bf16[64,128,128]{2,1,0:T(8,128)(2,1)} %get-tuple-element.13.contrib, f32[8,128,128]{2,1,0:T(8,128)} %get-tuple-element.14.local_h, f32[128,128]{1,0:T(8,128)} %get-tuple-element.15.w_local_h, s32[1,2,32]{2,1,0:T(2,128)} %bitcast.13, ...), custom_call_target="tpu_custom_call" | custom-call | tf_op jit(solution)/shard_map/pallas_call | solution.py:607
  93.7 0.7 copy.14
  94.4 0.6 copy.15

commit v5 on v4

--- a/solution.py
+++ b/solution.py
@@ -85,9 +85,6 @@
 
     up = chain((own, zp0, zp1), 0, 1)
     down = chain((own, zm0, zm1), 4, -1)
-    for n in range(2):
-        up[0][n].start()
-        down[0][n].start()
     asks = [
         pltpu.make_async_remote_copy(
             src_ref=need, dst_ref=pn_v.at[dy - 1],
@@ -103,7 +100,12 @@
         )
         for i, (dz, dy) in enumerate(FAR)
     ]
-    for copy in asks + far_asks:
+    for copy in asks:
+        copy.start()
+    for n in range(2):
+        up[0][n].start()
+        down[0][n].start()
+    for copy in far_asks:
         copy.start()
     loads[2].wait()
     for copy in asks:

time: 95.2 us -> 95.5 us (level)
    pallas_call x1, Pallas kernels: 7.64 us -> 10.5 us  [layer(): pl.pallas_call(layer_kernel, out_shape=(jax.ShapeDtypeStruct((BLK, TB, TB...]
    pallas_call x1, Pallas kernels: 40.7 us -> 38 us  [scatter(): pl.pallas_call(scatter_kernel, out_shape=(VMEM((BLK, TB, TB), bf), VMEM((...]
where the time goes in v5:
time: 95.5 us; the launch traced here: 95.2 us
  Pallas kernels  92.6 us (97%)
  local copies, waits for them, and re-layouts  1.33 us (1%)
  between operations  1.3 us (1%)
    pallas_call x1, Pallas kernels, gather(): pl.pallas_call(gather_kernel, out_shape=(jax.ShapeDtypeStruct((NSLOT, TB,...  44.1 us
    pallas_call x1, Pallas kernels, scatter(): pl.pallas_call(scatter_kernel, out_shape=(VMEM((BLK, TB, TB), bf), VMEM((...  38 us
    pallas_call x1, Pallas kernels, layer(): pl.pallas_call(layer_kernel, out_shape=(jax.ShapeDtypeStruct((BLK, TB, TB...  10.5 us

profile of v5, /device:TPU:2, one launch (start us, length us, event | category | flops | bytes accessed | tf_op | source)
XLA Modules:
  0.0 95.2 jit_solution(7648435577584493777)
XLA Ops:
  1.3 44.1 %shard_map.112 = (bf16[64,128,128]{2,1,0:T(8,128)(2,1)}, s32[3,1,2,32]{3,2,1,0:T(2,128)}) custom-call(bf16[8,128,128]{2,1,0:T(8,128)(2,1)} %bitcast.7, bf16[4,128,128]{2,1,0:T(8,128)(2,1)} %bitcast.9, s32[1,2,32]{2,1,0:T(2,128)} %bitcast.12), custom_call_target="tpu_custom_call" | custom-call | tf_op jit(solution)/shard_map/pallas_call | solution.py:199
  45.4 10.5 %shard_map.113 = (bf16[8,128,128]{2,1,0:T(8,128)(2,1)}, bf16[64,128,128]{2,1,0:T(8,128)(2,1)}, f32[8,128,128]{2,1,0:T(8,128)}, f32[128,128]{1,0:T(8,128)}) custom-call(s32[1,256]{1,0:T(1,128)} %row_h.1, s32[1,256]{1,0:T(1,128)} %col_h.1, s32[1]{0:T(128)S(6)} %copy.16.count_h, bf16[256,128,128]{2,1,0:T(8,128)(2,1)} %tiles_h.1, bf16[8,128,128]{2,1,0:T(8,128)(2,1)} %bitcast.8, ...), custom_call_target="tpu_custom_call" | custom-call | flops 2147483648 | bytes 16777216 | tf_op jit(solution)/shard_map/pallas_call | solution.py:368
  55.9 38.0 %shard_map.114 = (bf16[8,128,128]{2,1,0:T(8,128)(2,1)S(1)}, f32[128,128]{1,0:T(8,128)S(1)}) custom-call(bf16[64,128,128]{2,1,0:T(8,128)(2,1)} %get-tuple-element.13.contrib, f32[8,128,128]{2,1,0:T(8,128)} %get-tuple-element.14.local_h, f32[128,128]{1,0:T(8,128)} %get-tuple-element.15.w_local_h, s32[1,2,32]{2,1,0:T(2,128)} %bitcast.13, ...), custom_call_target="tpu_custom_call" | custom-call | tf_op jit(solution)/shard_map/pallas_call | solution.py:609
  93.9 0.7 copy.14
  94.6 0.6 copy.15
